TPU v7x, 32 devices: a whole 2x2x4 slice. The times are simulated.
32 devices in a mesh: expert: 4 (over y, core), fsdp: 8 (over z, x).
Axes of the slice: x: 2, y: 2, z: 4, core: 2. Of those that a mesh axis runs over, the one named last changes fastest.
Arguments:
- tokens: bfloat16 [4096, 2048], P(('expert', 'fsdp')), may hold values from -6 to 6
- expert_ids: int32 [4096, 4], P(('expert', 'fsdp')), may hold values from 0 to 7, all different within a row; in each aligned block of 128 rows (0 to 127, 128 to 255, ...) at most 128 rows name the same one
- w_query: float32 [2048, 2048], P(('expert', 'fsdp')), may hold values from -0.125 to 0.125
- b_query: float32 [2048], P(('expert', 'fsdp')), may hold values from -3 to 3
- w_key: float32 [2048, 2048], P(('expert', 'fsdp')), may hold values from -0.125 to 0.125
- b_key: float32 [2048], P(('expert', 'fsdp')), may hold values from -3 to 3
- w_value: float32 [2048, 2048], P(('expert', 'fsdp')), may hold values from -0.125 to 0.125
- b_value: float32 [2048], P(('expert', 'fsdp')), may hold values from -3 to 3
- w_output: float32 [2048, 2048], P(('expert', 'fsdp')), may hold values from -1 to 1
- attn_gain: float32 [2048], P(('expert', 'fsdp')), may hold values from 0.5 to 1.5
- ffn_gain: float32 [2048], P(('expert', 'fsdp')), may hold values from 0.5 to 1.5
- w_router: float32 [2048, 8], P(('expert', 'fsdp')), may hold values from -0.0625 to 0.0625
- shared_gate: float32 [2048], P(('expert', 'fsdp')), may hold values from -0.125 to 0.125
- shared_wgate: float32 [2048, 5632], P(('expert', 'fsdp')), may hold values from -0.125 to 0.125
- shared_wup: float32 [2048, 5632], P(('expert', 'fsdp')), may hold values from -0.125 to 0.125
- shared_wdown: float32 [5632, 2048], P(('expert', 'fsdp')), may hold values from -0.15625 to 0.15625
- expert_wgate: float32 [8, 2048, 1408], P('expert', 'fsdp'), may hold values from -0.125 to 0.125
- expert_wup: float32 [8, 2048, 1408], P('expert', 'fsdp'), may hold values from -0.125 to 0.125
- expert_wdown: float32 [8, 1408, 2048], P('expert', None, 'fsdp'), may hold values from -0.4375 to 0.4375
- cotangent: bfloat16 [4096, 2048], P(('expert', 'fsdp')), may hold values from -6 to 6
Outputs:
- output: bfloat16 [4096, 2048], P(('expert', 'fsdp'))
- token_grad: bfloat16 [4096, 2048], P(('expert', 'fsdp'))
- grad_w_query: float32 [2048, 2048], P(('expert', 'fsdp'))
- grad_b_query: float32 [2048], P(('expert', 'fsdp'))
- grad_w_key: float32 [2048, 2048], P(('expert', 'fsdp'))
- grad_b_key: float32 [2048], P(('expert', 'fsdp'))
- grad_w_value: float32 [2048, 2048], P(('expert', 'fsdp'))
- grad_b_value: float32 [2048], P(('expert', 'fsdp'))
- grad_w_output: float32 [2048, 2048], P(('expert', 'fsdp'))
- grad_attn_gain: float32 [2048], P(('expert', 'fsdp'))
- grad_ffn_gain: float32 [2048], P(('expert', 'fsdp'))
- grad_w_router: float32 [2048, 8], P(('expert', 'fsdp'))
- grad_shared_gate: float32 [2048], P(('expert', 'fsdp'))
- grad_shared_wgate: float32 [2048, 5632], P(('expert', 'fsdp'))
- grad_shared_wup: float32 [2048, 5632], P(('expert', 'fsdp'))
- grad_shared_wdown: float32 [5632, 2048], P(('expert', 'fsdp'))
- grad_expert_wgate: float32 [8, 2048, 1408], P('expert', 'fsdp')
- grad_expert_wup: float32 [8, 2048, 1408], P('expert', 'fsdp')
- grad_expert_wdown: float32 [8, 1408, 2048], P('expert', None, 'fsdp')
Inputs may be any that keep to these rules, and one draw needn't show every extreme that they name: `expert_ids`: each row names 4 different experts. Among the 128 rows of one device no expert is named more than 128 times, and in every draw some expert is named exactly 128 times by the rows of some device.
All inputs are finite; a program needn't handle non-finite values.
Results may differ from a plain program's by a relative error of at most 0.02.
The roundings to bfloat16 on the way count: a program that leaves them out, or rounds other values in their place, can miss the bound.
Values may be sent and summed in bfloat16 or wider, within the bound.
No kernel may reach another device: no remote copies, remote signals or barrier semaphores. Data moves between devices by JAX's collectives and lax.ppermute only.
A program may use at most 512 MiB of HBM per device.

v0:
```python
import jax
import jax.numpy as jnp
from jax import lax
from jax.sharding import PartitionSpec as P

HEADS = 16
HEAD_DIM = 128
HALF = HEAD_DIM // 2

E = "expert"
F = "fsdp"
EF = (E, F)

norm_eps = 1e-06
rope_base = 1000000.0
highest = lax.Precision.HIGHEST
bf16 = jnp.bfloat16
f32 = jnp.float32


def dot(left, right, left_dim, right_dim, precision=None):
    return lax.dot_general(
        left,
        right,
        (((left_dim,), (right_dim,)), ((), ())),
        precision=precision,
        preferred_element_type=f32,
    )


def product(left, right):
    return dot(left, right, 1, 0)


def product_t(left, right):
    return dot(left, right, 1, 1)


def contract(left, right):
    return dot(left, right, 0, 0)


def inverse_rms(rows):
    return lax.rsqrt(jnp.mean(rows * rows, axis=-1, keepdims=True) + norm_eps)


def norm_back(rows, gain, grad):
    factor = inverse_rms(rows)
    scaled = grad * gain
    along = jnp.mean(rows * scaled, axis=-1, keepdims=True)
    return factor * scaled - rows * (factor * factor * factor * along), rows * factor


def rope_tables(places):
    places = places.astype(f32)
    frequency = rope_base ** (-(jnp.arange(HALF, dtype=jnp.int32).astype(f32) * 2.0 / HEAD_DIM))
    angles = places[:, None] * frequency[None, :]
    cosine, sine = jnp.cos(angles), jnp.sin(angles)
    return jnp.concatenate([cosine, cosine], axis=1), jnp.concatenate([-sine, sine], axis=1)


def swap(head):
    return jnp.concatenate([head[:, HALF:], head[:, :HALF]], axis=1)


def ring_order(size):
    levels = 4 if size % 4 == 0 else size
    across = size // levels
    return [
        level * across + at
        for at in range(across)
        for level in (range(levels) if at % 2 == 0 else reversed(range(levels)))
    ]


def ring_shift(size, by):
    order = ring_order(size)
    return [(order[i], order[(i + by) % size]) for i in range(size)]


def ring_neighbour(by):
    size = lax.axis_size(F)
    order = ring_order(size)
    places = [order.index(f) for f in range(size)]
    at = jnp.array(places, jnp.int32)[lax.axis_index(F)]
    return jnp.array(order, jnp.int32)[(at + by) % size]


def ring_gather(shard, ties=None):
    ties = ties or {}
    size = lax.axis_size(F)
    right, left = ring_shift(size, 1), ring_shift(size, -1)
    rows = shard.shape[0]
    cut = rows // 2
    whole = jnp.zeros((size * rows,) + shard.shape[1:], shard.dtype)

    def put(whole, block, by, first=0):
        return lax.dynamic_update_slice_in_dim(
            whole, block, ring_neighbour(by) * rows + first, 0
        )

    up = down = shard
    whole = put(whole, shard, 0)
    for step in range(1, size // 2):
        up, down = tied(up, down, ties.get(step))
        up, down = lax.ppermute(up, F, right), lax.ppermute(down, F, left)
        whole = put(put(whole, up, -step), down, step)
    up, down = tied(up, down, ties.get(size // 2))
    up, down = lax.ppermute(up[:cut], F, right), lax.ppermute(down[cut:], F, left)
    return put(put(whole, up, size // 2), down, size // 2, cut)


def ring_scatter(terms, ties=None):
    ties = ties or {}
    size = lax.axis_size(F)
    right, left = ring_shift(size, 1), ring_shift(size, -1)
    half = size // 2
    rows = terms.shape[0] // size
    cut = rows // 2

    def block(by):
        return lax.dynamic_slice_in_dim(terms, ring_neighbour(by) * rows, rows, 0)

    opposite = block(half).astype(bf16)
    up, down = opposite[:cut], opposite[cut:]
    for step in range(half - 1, 0, -1):
        up, down = lax.ppermute(up, F, right), lax.ppermute(down, F, left)
        plus, minus = block(step).astype(f32), block(-step).astype(f32)
        if step == half - 1:
            plus = jnp.concatenate([plus[:cut] + up.astype(f32), plus[cut:]])
            minus = jnp.concatenate([minus[:cut], minus[cut:] + down.astype(f32)])
        else:
            plus, minus = plus + up.astype(f32), minus + down.astype(f32)
        up, down = tied(plus.astype(bf16), minus.astype(bf16), ties.get(step))
    up, down = lax.ppermute(up, F, right), lax.ppermute(down, F, left)
    up, down = tied(up, down, ties.get(0))
    return block(0).astype(f32) + up.astype(f32) + down.astype(f32)


def tied(up, down, tie):
    if tie is None:
        return up, down
    return lax.optimization_barrier((up, down, tie))[:2]


def pick(blocks, index):
    return lax.dynamic_index_in_dim(blocks, index, 0, keepdims=False)


def swap_blocks(blocks, axis):
    return lax.all_to_all(blocks, axis, split_axis=0, concat_axis=0, tiled=True)


def sibling(value):
    return lax.ppermute(value, E, [(e, e ^ 1) for e in range(lax.axis_size(E))])


def along_y(value, by):
    size = lax.axis_size(E)
    return lax.ppermute(value, E, [(e, (e + 2 * by) % size) for e in range(size)])


def gather_e(block):
    size, at = lax.axis_size(E), lax.axis_index(E)
    levels, rows = size // 2, block.shape[0]
    whole = jnp.zeros((size * rows,) + block.shape[1:], block.dtype)
    for by in range(levels):
        came = along_y(block, by) if by else block
        source = 2 * ((at // 2 - by) % levels) + at % 2
        whole = lax.dynamic_update_slice_in_dim(whole, came, source * rows, 0)
        whole = lax.dynamic_update_slice_in_dim(whole, sibling(came), (source ^ 1) * rows, 0)
    return whole


def reduce_e(blocks):
    size, at = lax.axis_size(E), lax.axis_index(E)
    levels, core = size // 2, at % 2
    blocks = blocks.reshape((levels, 2) + blocks.shape[1:])
    mine = lax.dynamic_index_in_dim(blocks, core, 1, keepdims=False)
    theirs = lax.dynamic_index_in_dim(blocks, 1 - core, 1, keepdims=False)
    mine = mine + sibling(theirs.astype(bf16)).astype(f32)
    total = pick(mine, at // 2)
    for by in range(1, levels):
        total = total + along_y(pick(mine, (at // 2 + by) % levels).astype(bf16), by).astype(f32)
    return total


def after(value, *others):
    return lax.optimization_barrier((value,) + others)[0]


def shards(
    tokens,
    expert_ids,
    w_query,
    b_query,
    w_key,
    b_key,
    w_value,
    b_value,
    w_output,
    attn_gain,
    ffn_gain,
    w_router,
    shared_gate,
    shared_wgate,
    shared_wup,
    shared_wdown,
    expert_wgate,
    expert_wup,
    expert_wdown,
    cotangent,
):
    n_e, n_f = lax.axis_size(E), lax.axis_size(F)
    devices = n_e * n_f
    at_e, at_f = lax.axis_index(E), lax.axis_index(F)
    rows, width = tokens.shape
    seq = rows * n_f
    slab = width // n_f
    part = width // devices
    heads = HEADS // n_f
    experts, top = w_router.shape[1], expert_ids.shape[1]
    own = experts // n_e
    per_expert = expert_wgate.shape[2] // n_f
    per_shared = shared_wdown.shape[0]
    hidden_own = own * per_expert + per_shared
    score_scale = HEAD_DIM ** (-0.5)

    small = jnp.concatenate(
        [
            jnp.stack([b_query, b_key, b_value, attn_gain, ffn_gain, shared_gate]).astype(bf16),
            w_router.T.astype(bf16),
            expert_ids.T.astype(bf16).reshape(-1, part),
        ]
    )
    small_all = swap_blocks(jnp.broadcast_to(small, (devices,) + small.shape), EF)
    vectors = small_all[:, : 6 + experts].transpose(1, 0, 2).reshape(6 + experts, width)
    ids_all = small_all[:, 6 + experts :].reshape(n_e, n_f, top, rows)

    def ids_of(e):
        return pick(ids_all, e).transpose(0, 2, 1).reshape(seq, top)

    biases = lax.dynamic_slice_in_dim(vectors[:3], at_f * slab, slab, 1).astype(f32)
    gain_one = vectors[3].astype(f32)
    gain_two = vectors[4].astype(f32)
    route_rows = vectors[5:]

    w_out = lax.all_gather(w_output.astype(bf16), EF, axis=0, tiled=True)
    qkv_own = jnp.stack([w_query, w_key, w_value]).astype(bf16).reshape(3, part, n_f, slab)
    qkv_own = swap_blocks(qkv_own.transpose(2, 1, 0, 3).reshape(n_f, part, 3 * slab), F)
    w_qkv = gather_e(qkv_own.reshape(n_f * part, 3 * slab))

    def by_hidden(expert_weight, shared_weight):
        routed = expert_weight.astype(bf16).transpose(0, 2, 1).reshape(own, n_f, per_expert, slab)
        routed = routed.transpose(1, 0, 2, 3).reshape(n_f, own * per_expert, slab)
        shared = shared_weight.T.reshape(n_f, per_shared, slab)
        return jnp.concatenate([routed, shared], axis=1)

    shared_two = jnp.stack([shared_wgate, shared_wup]).astype(bf16)
    shared_two = shared_two.reshape(2, part, n_e, n_f * per_shared).transpose(2, 0, 1, 3)
    shared_two = swap_blocks(shared_two.reshape(n_e, 2 * part, n_f * per_shared), E)
    shared_two = shared_two.reshape(n_e, 2, part, n_f * per_shared).transpose(1, 0, 2, 3)
    shared_two = shared_two.reshape(2, n_e * part, n_f * per_shared)
    gate_blocks = by_hidden(expert_wgate, shared_two[0])
    up_blocks = by_hidden(expert_wup, shared_two[1])
    routed_down = expert_wdown.astype(bf16).reshape(own, n_f, per_expert, slab)
    routed_down = routed_down.transpose(1, 0, 2, 3).reshape(n_f, own * per_expert, slab)

    def full_width(blocks):
        return blocks.transpose(1, 0, 2).reshape(blocks.shape[1], width)

    def gate_like(mine):
        routed = full_width(mine[:, : own * per_expert])
        shared = mine[:, own * per_expert :].reshape(n_f, per_shared, n_e, part)
        shared = shared.transpose(1, 2, 0, 3).reshape(per_shared, width)
        return jnp.concatenate([routed, shared])

    def both_levels(mine):
        return jnp.concatenate([mine] + [along_y(mine, by) for by in range(1, levels)])

    levels = n_e // 2
    x_all = ring_gather(tokens, {n_f // 2: (qkv_own, gate_blocks, up_blocks, routed_down)})
    gate_mine = swap_blocks(after(gate_blocks, x_all), F)
    up_mine = swap_blocks(after(up_blocks, x_all), F)

    blocks = own + 1
    column = jnp.arange(levels * hidden_own, dtype=jnp.int32)
    level_of = (at_e // 2 - column // hidden_own) % levels
    block_of = (2 * level_of + at_e % 2) * blocks + jnp.minimum(
        (column % hidden_own) // per_expert, own
    )
    spread = (jnp.arange(n_e * blocks, dtype=jnp.int32)[:, None] == block_of[None, :]).astype(f32)

    x_wide = x_all.astype(f32)
    x_hat = x_wide * inverse_rms(x_wide)
    normed = (x_hat * gain_one).astype(bf16)
    places = jnp.arange(seq, dtype=jnp.int32)
    cosine, sine = rope_tables(places)
    lin = product(normed, w_qkv)
    causal = places[:, None] >= places[None, :]
    saved, mixed_parts = [], []
    for h in range(heads):
        at = h * HEAD_DIM
        q_lin, k_lin, v_lin = [
            lin[:, i * slab + at : i * slab + at + HEAD_DIM] + biases[i, at : at + HEAD_DIM]
            for i in range(3)
        ]
        q = ((q_lin * cosine + swap(q_lin) * sine) * score_scale).astype(bf16)
        k = (k_lin * cosine + swap(k_lin) * sine).astype(bf16)
        v = v_lin.astype(bf16)
        scores = jnp.where(causal, product_t(q, k), -1e30)
        top_score = jnp.max(scores, axis=-1, keepdims=True)
        log_total = top_score + jnp.log(
            jnp.sum(jnp.exp(scores - top_score), axis=-1, keepdims=True)
        )
        probs = jnp.exp(scores - log_total)
        mixed_parts.append(product(probs.astype(bf16), v).astype(bf16))
        saved.append((q, k, v, probs))
    mixed = jnp.concatenate(mixed_parts, axis=1)
    gate_mine = gate_like(after(gate_mine, mixed))
    w_gate = both_levels(gate_mine)
    mixed_own = swap_blocks(mixed.reshape(n_f, rows, slab), F)
    up_mine = gate_like(after(up_mine, mixed_own))
    mixed_own = mixed_own.transpose(1, 0, 2).reshape(rows, width)
    hidden = tokens.astype(f32) + product(mixed_own, w_out)

    ffn_own = (hidden * inverse_rms(hidden) * gain_two).astype(bf16)
    w_up = both_levels(up_mine)
    g_all = lax.all_gather(after(cotangent, mixed_own), F, axis=0, tiled=True)
    g_both = jnp.concatenate([g_all, sibling(g_all)])
    down_mine = swap_blocks(after(routed_down, mixed_own), F)
    ffn_all = ring_gather(after(ffn_own, up_mine))
    ffn_both = jnp.concatenate([ffn_all, sibling(ffn_all)])
    down_mine = full_width(after(down_mine, ffn_all))
    down_mine = jnp.concatenate([down_mine, shared_wdown.astype(bf16)])
    w_down = both_levels(down_mine)

    named = jnp.arange(experts, dtype=jnp.int32).astype(bf16)
    ids = jnp.concatenate([ids_of(at_e), ids_of(at_e ^ 1)])
    selected = jnp.sum((ids[:, :, None] == named).astype(f32), axis=1)
    logits = product_t(ffn_both, route_rows)
    logit_exp = jnp.exp(logits[:, 1:] - jnp.max(logits[:, 1:], axis=-1, keepdims=True))
    route_probs = logit_exp / jnp.sum(logit_exp, axis=-1, keepdims=True)
    shared_scale = jax.nn.sigmoid(logits[:, :1])
    gates = jnp.concatenate(
        [
            (route_probs * selected).reshape(2 * seq, n_e, own),
            jnp.broadcast_to(shared_scale[:, None, :], (2 * seq, n_e, 1)),
        ],
        axis=2,
    ).reshape(2 * seq, n_e * blocks)
    scale = dot(gates, spread, 1, 0, highest)
    pre_gate = product_t(ffn_both, w_gate)
    pre_up = product_t(ffn_both, w_up)
    sig = jax.nn.sigmoid(pre_gate)
    silu = pre_gate * sig
    slope = sig * (1.0 + pre_gate * (1.0 - sig))
    mid = (silu * pre_up).astype(bf16).astype(f32)
    mid_scaled = (mid * scale).astype(bf16)

    def over_levels(grad):
        total = grad[:hidden_own].astype(f32)
        for by in range(1, levels):
            there = grad[by * hidden_own : (by + 1) * hidden_own]
            total = total + along_y(there, -by).astype(f32)
        return total.astype(bf16)

    d_down_all = contract(mid_scaled, after(g_both, down_mine)).astype(bf16)
    d_down = over_levels(d_down_all)

    mid_grad = product_t(after(g_both, d_down_all), w_down)
    sums = dot(spread, mid * mid_grad, 1, 1, highest)
    scaled = mid_grad * scale
    gate_grad = (scaled * pre_up * slope).astype(bf16)
    up_grad = (scaled * silu).astype(bf16)

    def input_grad(first):
        rows_of = slice(first, first + seq)
        return product(gate_grad[rows_of], w_gate) + product(up_grad[rows_of], w_up)

    from_sibling = sibling(input_grad(seq).astype(bf16))
    moe_sibling = sibling(product(mid_scaled[seq:], w_down).astype(bf16))
    gate_sums = sums[:, :seq] + sibling(sums[:, seq:])
    gate_sums = gate_sums.reshape(n_e * blocks, n_f, rows).transpose(1, 0, 2)
    gate_sums = jnp.sum(swap_blocks(gate_sums, F), axis=0)
    d_gate_all = contract(gate_grad, ffn_both).astype(bf16)
    d_up_all = contract(up_grad, ffn_both).astype(bf16)
    d_gate, d_up = over_levels(d_gate_all), over_levels(d_up_all)
    moe = (product(mid_scaled[:seq], w_down) + moe_sibling.astype(f32)).astype(bf16)
    ffn_grad = ring_scatter(
        (input_grad(0) + from_sibling.astype(f32)).astype(bf16),
        {3: d_gate_all, 2: d_up_all, 1: moe, 0: gate_sums},
    )
    moe = lax.psum_scatter(moe, F, scatter_dimension=0, tiled=True)
    output = (hidden + moe.astype(f32)).astype(bf16)
    gate_sums = gate_sums.T.reshape(rows, n_e, blocks)

    def mine(table):
        return lax.dynamic_slice_in_dim(table, at_f * rows, rows, 0)

    probs_own, shared_own, selected_own = mine(route_probs), mine(shared_scale), mine(selected)
    prob_grad = gate_sums[:, :, :own].reshape(rows, experts) * selected_own
    logit_grad = probs_own * (
        prob_grad - jnp.sum(probs_own * prob_grad, axis=-1, keepdims=True)
    )
    weight_grad = (
        jnp.sum(gate_sums[:, :, own], axis=1, keepdims=True) * shared_own * (1.0 - shared_own)
    )
    route_grad = jnp.concatenate([weight_grad, logit_grad], axis=1)
    d_route = dot(route_grad, ffn_own.astype(f32), 0, 0, highest)
    ffn_grad = ffn_grad + dot(route_grad, route_rows.astype(f32), 1, 0, highest)
    hidden_back, hidden_hat = norm_back(hidden, gain_two, ffn_grad)
    d_gain_two = jnp.sum(ffn_grad * hidden_hat, axis=0)
    hidden_grad = cotangent.astype(f32) + hidden_back

    def by_slab(grad):
        return grad.reshape(grad.shape[0], n_f, slab).transpose(1, 0, 2)

    def gate_slabs(grad):
        routed, shared = grad[: own * per_expert], grad[own * per_expert :]
        shared = shared.reshape(per_shared, n_e, n_f, part).transpose(2, 0, 1, 3)
        shared = shared.reshape(n_f, per_shared, slab)
        return jnp.concatenate([by_slab(routed), shared], axis=1)

    hidden_low = hidden_grad.astype(bf16)
    mixed_grad = product_t(hidden_low, w_out).astype(bf16).reshape(rows, n_f, slab)
    mixed_grad = swap_blocks(mixed_grad.transpose(1, 0, 2), F)
    d_down_back = swap_blocks(by_slab(d_down[: own * per_expert]), F)
    gate_back = swap_blocks(gate_slabs(d_gate), F)
    up_back = swap_blocks(gate_slabs(d_up), F)
    mixed_grad = mixed_grad.reshape(seq, slab)
    hidden_low = lax.all_gather(hidden_low, F, axis=0, tiled=True)
    d_out = contract(mixed, hidden_low)
    lin_grads = [[], [], []]
    for h in range(heads):
        q, k, v, probs = saved[h]
        out_grad = mixed_grad[:, h * HEAD_DIM : (h + 1) * HEAD_DIM]
        p_grad = product_t(out_grad, v)
        delta = jnp.sum(probs * p_grad, axis=-1, keepdims=True)
        s_grad = (probs * (p_grad - delta)).astype(bf16)
        dq = product(s_grad, k) * score_scale
        dk = contract(s_grad, q)
        lin_grads[0].append((dq * cosine - swap(dq) * sine).astype(bf16))
        lin_grads[1].append((dk * cosine - swap(dk) * sine).astype(bf16))
        lin_grads[2].append(contract(probs.astype(bf16), out_grad).astype(bf16))
    lin_grad = jnp.concatenate(lin_grads[0] + lin_grads[1] + lin_grads[2], axis=1)
    normed_part = product_t(lin_grad, w_qkv).astype(bf16)
    d_qkv = contract(normed, lin_grad)
    normed_grad = ring_scatter(normed_part, {3: d_qkv, 1: d_down_back, 0: gate_back})
    d_bias = jnp.sum(lin_grad.astype(f32), axis=0).reshape(3, slab)
    d_gain_one = jnp.sum(d_qkv * w_qkv.astype(f32), axis=1) / gain_one
    token_back, unused = norm_back(tokens.astype(f32), gain_one, normed_grad)
    token_grad = (hidden_grad + token_back).astype(bf16)

    def return_routed(back):
        back = back.reshape(n_f, own, per_expert, slab).transpose(1, 0, 2, 3)
        return back.reshape(own, n_f * per_expert, slab)

    def return_gate(back):
        return return_routed(back[:, : own * per_expert]).transpose(0, 2, 1).astype(f32)

    d_shared_down = d_down[own * per_expert :].astype(f32)
    d_expert_down = return_routed(d_down_back).astype(f32)
    d_expert_gate, d_expert_up = return_gate(gate_back), return_gate(up_back)
    shared_two = jnp.stack([gate_back[:, own * per_expert :], up_back[:, own * per_expert :]])
    shared_two = shared_two.reshape(2, n_f * per_shared, slab).transpose(0, 2, 1)
    shared_two = shared_two.reshape(2, n_e, part, n_f * per_shared).transpose(1, 0, 2, 3)
    shared_two = swap_blocks(shared_two.reshape(n_e, 2 * part, n_f * per_shared), E)
    shared_two = shared_two.reshape(n_e, 2, part, n_f * per_shared).transpose(1, 2, 0, 3)
    shared_two = shared_two.reshape(2, part, devices * per_shared).astype(f32)

    from_heads = [(e * n_f + f, n_e * f + e) for e in range(n_e) for f in range(n_f)]
    d_out = reduce_e(d_out.reshape(n_e, part, width)).astype(bf16)
    d_wout = lax.ppermute(d_out, EF, from_heads).astype(f32)
    d_qkv = reduce_e(d_qkv.reshape(n_e, n_f * part, 3 * slab)).astype(bf16)
    d_qkv = swap_blocks(d_qkv.reshape(n_f, part, 3 * slab), F)
    d_qkv = d_qkv.reshape(n_f, part, 3, slab).transpose(2, 1, 0, 3).reshape(3, part, width)
    d_qkv = d_qkv.astype(f32)

    bias_rows = lax.dynamic_update_slice_in_dim(
        jnp.zeros((3, width), f32), d_bias, at_f * slab, 1
    )
    d_small = jnp.concatenate([bias_rows, d_gain_one[None], d_gain_two[None], d_route])
    d_small = d_small.reshape(6 + experts, n_e, n_f, part).transpose(2, 1, 0, 3)
    d_small = jnp.sum(swap_blocks(d_small, F), axis=0)
    d_small = jnp.sum(swap_blocks(d_small, E), axis=0)

    return (
        output,
        token_grad,
        d_qkv[0],
        d_small[0],
        d_qkv[1],
        d_small[1],
        d_qkv[2],
        d_small[2],
        d_wout,
        d_small[3],
        d_small[4],
        d_small[6:].T,
        d_small[5],
        shared_two[0],
        shared_two[1],
        d_shared_down,
        d_expert_gate,
        d_expert_up,
        d_expert_down,
    )


def solution(mesh):
    matrix, vector = P(EF, None), P(EF)
    wide, tall = P(E, F, None), P(E, None, F)
    in_specs = (matrix, matrix) + (matrix, vector) * 3 + (matrix, vector, vector, matrix, vector)
    in_specs = in_specs + (matrix,) * 3 + (wide, wide, tall, matrix)
    out_specs = (matrix, matrix) + (matrix, vector) * 3 + (matrix, vector, vector, matrix, vector)
    out_specs = out_specs + (matrix,) * 3 + (wide, wide, tall)
    return jax.shard_map(shards, mesh=mesh, in_specs=in_specs, out_specs=out_specs, check_vma=False)
```

profile of v0, /device:TPU:1, one launch (start us, length us, event | category | flops | bytes accessed | tf_op | source)
XLA Modules:
  0.0 1119.3 jit_solution(11004980156339284788)
XLA Ops:
  76.8 25.9 %collective-permute-done.3 = bf16[128,2048]{1,0:T(8,128)(2,1)} collective-permute-done((bf16[128,2048]{1,0:T(8,128)(2,1)}, bf16[128,2048]{1,0:T(8,128)(2,1)}, u32[]{:S(2)}, u32[]{:S(2)}) %collective-permute-start.3) | collective-permute-done | bytes 524320 | tf_op jit(solution)/shard_map/ppermute | solution.py:106
  158.8 16.9 %all_to_all.80 = bf16[8,128,256]{1,2,0:T(8,128)(2,1)S(1)} all-to-all(bf16[8,128,256]{1,2,0:T(8,128)(2,1)S(1)} %copy_bitcast_fusion), channel_id=1, replica_groups=mesh['expert'=4,'fsdp'=8] {'fsdp'}, dimensions={0} | all-to-all | bytes 1048576 | tf_op jit(solution)/shard_map/all_to_all | solution.py:151
  179.8 76.1 %all-to-all-done.4 = bf16[8,528,256]{2,1,0:T(8,128)(2,1)S(1)} async-done(((bf16[8,528,256]{2,1,0:T(8,128)(2,1)}), bf16[8,528,256]{2,1,0:T(8,128)(2,1)S(1)}, u32[]{:S(2)}, u32[]{:S(2)}) %all-to-all-start.4) | async-done | bytes 2162720 | tf_op jit(solution)/shard_map/all_to_all | solution.py:151
  280.9 9.2 collective-permute-done.12
  291.8 8.4 collective-permute-start.24
  305.4 19.1 %collective-permute-done.14 = bf16[128,2048]{1,0:T(8,128)(2,1)} collective-permute-done((bf16[128,2048]{1,0:T(8,128)(2,1)S(1)}, bf16[128,2048]{1,0:T(8,128)(2,1)}, u32[]{:S(2)}, u32[]{:S(2)}) %collective-permute-start.14) | collective-permute-done | bytes 524320 | tf_op jit(solution)/shard_map/ppermute | solution.py:106
  331.7 19.4 %collective-permute-start.15 = (bf16[128,2048]{1,0:T(8,128)(2,1)}, bf16[128,2048]{1,0:T(8,128)(2,1)S(1)}, u32[]{:S(2)}, u32[]{:S(2)}) collective-permute-start(bf16[128,2048]{1,0:T(8,128)(2,1)} %collective-permute-done.13), channel_id=1, source_target_pairs={{0,2},{2,4},{4,6},{6,7},{7,5},{5,3},{3,1},{1,0},{8,10},{10,12},{12... | collective-permute-start | bytes 1572872 | tf_op jit(solution)/shard_map/ppermute | solution.py:106
  394.3 17.0 %all-to-all-done.6 = bf16[8,352,256]{2,1,0:T(8,128)(2,1)} async-done(((bf16[8,352,256]{2,1,0:T(8,128)(2,1)}), bf16[8,352,256]{2,1,0:T(8,128)(2,1)}, u32[]{:S(2)}, u32[]{:S(2)}) %all-to-all-start.6) | async-done | bytes 1441824 | tf_op jit(solution)/shard_map/all_to_all | solution.py:151
  421.3 9.6 collective-permute-done.21
  430.9 14.6 %fusion.130 = f32[2048,1056]{0,1:T(8,128)} fusion(bf16[528,2048]{1,0:T(8,128)(2,1)} %collective-permute-done.21, bf16[176,2048]{1,0:T(8,128)(2,1)} %copy-done.34, bf16[352,2048]{1,0:T(8,128)(2,1)S(1)} %bitcast.329, bf16[1024,2048]{1,0:T(8,128)(2,1)} %collective-permute-done.19, bf16[1024,2048]{1,0:T(8,128)(2,1)} %constant_dynamic-update-slice_fusion.5), kind=kOutput, calls=%fused_computation.337 | convolution fusion | flops 8888123392 | bytes 21364736 | tf_op jit(solution)/shard_map/dot_general | solution.py:22
  445.5 31.7 %collective-permute-done.20 = bf16[528,2048]{1,0:T(8,128)(2,1)} collective-permute-done((bf16[528,2048]{1,0:T(8,128)(2,1)}, bf16[528,2048]{1,0:T(8,128)(2,1)}, u32[]{:S(2)}, u32[]{:S(2)}) %collective-permute-start.20) | collective-permute-done | bytes 2162720 | tf_op jit(solution)/shard_map/ppermute | solution.py:160
  477.2 14.7 %fusion.131 = f32[2048,1056]{0,1:T(8,128)} fusion(bf16[528,2048]{1,0:T(8,128)(2,1)} %collective-permute-done.20, bf16[176,2048]{1,0:T(8,128)(2,1)S(1)} %copy-done.37, bf16[352,2048]{1,0:T(8,128)(2,1)S(1)} %bitcast.339, bf16[1024,2048]{1,0:T(8,128)(2,1)} %collective-permute-done.19, bf16[1024,2048]{1,0:T(8,128)(2,1)} %constant_dynamic-update-slice_fusion.5), kind=kOutput, calls=%fused_computation.338 | convolution fusion | flops 8888123392 | bytes 21364736 | tf_op jit(solution)/shard_map/dot_general | solution.py:22
  491.9 12.0 %fusion = (bf16[2048,1056]{0,1:T(8,128)(2,1)S(1)}, bf16[2048,1056]{0,1:T(8,128)(2,1)}, f32[2048,1056]{0,1:T(8,128)}) fusion(f32[2048,1056]{0,1:T(8,128)} %fusion.130, f32[2048,1056]{0,1:T(8,128)} %fusion.131, f32[2048,12]{0,1:T(8,128)S(1)} %reshape.580, s32[1056]{0:T(1024)S(1)} %fusion.97), kind=kOutput, calls=%fused_computation.4 | convolution fusion | flops 330903936 | bytes 34705536 | tf_op jit(solution)/shard_map/dot_general | solution.py:22
  504.0 13.1 %convolution_convert_fusion.2 = bf16[1056,2048]{1,0:T(8,128)(2,1)S(1)} fusion(bf16[2048,1056]{0,1:T(8,128)(2,1)S(1)} %get-tuple-element.190, bf16[2048,2048]{1,0:T(8,128)(2,1)} %constant_dynamic-update-slice_fusion), kind=kOutput, calls=%fused_computation.20 | convolution fusion | flops 8860532736 | bytes 17039360 | tf_op jit(solution)/shard_map/dot_general | solution.py:22
  523.6 9.1 convolution_convert_fusion.4
  533.4 24.4 %multiply_convert_fusion.1 = (bf16[2048,1056]{0,1:T(8,128)(2,1)}, bf16[2048,1056]{0,1:T(8,128)(2,1)}, f32[2048,1056]{0,1:T(8,128)}) fusion(f32[2048,1056]{0,1:T(8,128)} %fusion.131, f32[2048,1056]{0,1:T(8,128)} %fusion.130, f32[2048,1056]{0,1:T(8,128)} %get-tuple-element.282, bf16[2048,2048]{1,0:T(8,128)(2,1)} %constant_dynamic-update-slice_fusion, ...), kind=kOutput, calls=%fused_computation.7 | convolution fusion | flops 8901623808 | bytes 55967744 | tf_op jit(solution)/shard_map/dot_general | solution.py:22
  566.8 12.0 %convolution_convert_fusion.1 = bf16[1056,2048]{1,0:T(8,128)(2,1)S(1)} fusion(bf16[2048,1056]{0,1:T(8,128)(2,1)S(1)} %copy-done.85, bf16[1024,2048]{1,0:T(8,128)(2,1)} %collective-permute-done.19, bf16[1024,2048]{1,0:T(8,128)(2,1)} %constant_dynamic-update-slice_fusion.5), kind=kOutput, calls=%fused_computation.19 | convolution fusion | flops 8877309952 | bytes 17039360 | tf_op jit(solution)/shard_map/dot_general | solution.py:22
  588.5 9.3 add_convert_fusion.1
  598.8 13.2 %convolution_convert_fusion = bf16[1056,2048]{1,0:T(8,128)(2,1)} fusion(bf16[2048,1056]{0,1:T(8,128)(2,1)S(1)} %bitcast.413, bf16[1024,2048]{1,0:T(8,128)(2,1)} %collective-permute-done.19, bf16[1024,2048]{1,0:T(8,128)(2,1)} %constant_dynamic-update-slice_fusion.5), kind=kOutput, calls=%fused_computation.18 | convolution fusion | flops 8877309952 | bytes 17039360 | tf_op jit(solution)/shard_map/dot_general | solution.py:22
  612.0 9.8 fusion.17
  627.8 9.7 fusion.15
  639.0 11.5 %add_convert_fusion = bf16[1024,2048]{1,0:T(8,128)(2,1)} fusion(bf16[1024,2048]{1,0:T(8,128)(2,1)} %collective-permute-done.25, f32[1024,2048]{1,0:T(8,128)} %fusion.17, f32[1024,2048]{1,0:T(8,128)} %fusion.15), kind=kLoop, calls=%fused_computation.15 | loop fusion | flops 8388608 | bytes 25165824 | tf_op jit(solution)/shard_map/convert_element_type | solution.py:391
  679.8 10.1 add_convert_fusion.2
  689.8 18.9 %collective-permute-done.30 = bf16[128,2048]{1,0:T(8,128)(2,1)} collective-permute-done((bf16[128,2048]{1,0:T(8,128)(2,1)}, bf16[128,2048]{1,0:T(8,128)(2,1)}, u32[]{:S(2)}, u32[]{:S(2)}) %collective-permute-start.30) | collective-permute-done | bytes 524320 | tf_op jit(solution)/shard_map/ppermute | solution.py:127
  711.6 10.4 collective-permute-start.32
  748.6 46.1 %collective-permute-done.50 = bf16[528,2048]{1,0:T(8,128)(2,1)S(1)} collective-permute-done((bf16[528,2048]{1,0:T(8,128)(2,1)S(1)}, bf16[528,2048]{1,0:T(8,128)(2,1)S(1)}, u32[]{:S(2)}, u32[]{:S(2)}) %collective-permute-start.50) | collective-permute-done | bytes 2162720 | tf_op jit(solution)/shard_map/ppermute | solution.py:160
  827.5 61.8 %all-to-all-done.14 = bf16[8,528,256]{2,1,0:T(8,128)(2,1)} async-done(((bf16[8,528,256]{2,1,0:T(8,128)(2,1)}), bf16[8,528,256]{2,1,0:T(8,128)(2,1)}, u32[]{:S(2)}, u32[]{:S(2)}) %all-to-all-start.14) | async-done | bytes 2162720 | tf_op jit(solution)/shard_map/all_to_all | solution.py:151
  946.8 9.8 multiply_reduce_fusion
  995.5 11.6 %all-to-all-done.12 = f32[8,1,3584]{2,1,0:T(1,128)} async-done(((f32[8,1,3584]{2,1,0:T(1,128)}), f32[8,1,3584]{2,1,0:T(1,128)}, u32[]{:S(2)}, u32[]{:S(2)}) %all-to-all-start.12) | async-done | bytes 114720 | tf_op jit(solution)/shard_map/all_to_all | solution.py:151
  1030.4 11.9 %collective-permute-done.46 = bf16[512,768]{1,0:T(8,128)(2,1)} collective-permute-done((bf16[512,768]{1,0:T(8,128)(2,1)S(1)}, bf16[512,768]{1,0:T(8,128)(2,1)}, u32[]{:S(2)}, u32[]{:S(2)}) %collective-permute-start.46) | collective-permute-done | bytes 786464 | tf_op jit(solution)/shard_map/ppermute | solution.py:160
  1059.5 12.3 %collective-permute-done.42 = bf16[128,2048]{1,0:T(8,128)(2,1)} collective-permute-done((bf16[128,2048]{1,0:T(8,128)(2,1)}, bf16[128,2048]{1,0:T(8,128)(2,1)}, u32[]{:S(2)}, u32[]{:S(2)}) %collective-permute-start.42) | collective-permute-done | bytes 524320 | tf_op jit(solution)/shard_map/ppermute | solution.py:135
  1095.5 16.0 %collective-permute-done.49 = bf16[64,2048]{1,0:T(8,128)(2,1)S(1)} collective-permute-done((bf16[64,2048]{1,0:T(8,128)(2,1)}, bf16[64,2048]{1,0:T(8,128)(2,1)S(1)}, u32[]{:S(2)}, u32[]{:S(2)}) %collective-permute-start.49) | collective-permute-done | bytes 262176 | tf_op jit(solution)/shard_map/ppermute | solution.py:474
  (593 shorter events, 495.5 us)
Async XLA Ops:
  7.2 257.8 %all-gather.4.cloned.1.call-start = ((), (), s32[]{:S(2)}) async-start(), calls=%async_computation.17 | async-start | bytes 8650752 | tf_op jit(solution)/shard_map/all_gather | solution.py:248
  9.1 58.2 %collective-permute-start.1 = (bf16[128,2048]{1,0:T(8,128)(2,1)}, bf16[128,2048]{1,0:T(8,128)(2,1)}, u32[]{:S(2)}, u32[]{:S(2)}) collective-permute-start(bf16[128,2048]{1,0:T(8,128)(2,1)} %param.88), channel_id=1, source_target_pairs={{0,1},{2,0},{4,2},{6,4},{7,6},{5,7},{3,5},{1,3},{8,9},{10,8},{12,1... | collective-permute-start | bytes 1572872 | tf_op jit(solution)/shard_map/ppermute | solution.py:106
  11.2 56.6 %collective-permute-start = (bf16[128,2048]{1,0:T(8,128)(2,1)}, bf16[128,2048]{1,0:T(8,128)(2,1)}, u32[]{:S(2)}, u32[]{:S(2)}) collective-permute-start(bf16[128,2048]{1,0:T(8,128)(2,1)} %param.88), channel_id=1, source_target_pairs={{0,2},{2,4},{4,6},{6,7},{7,5},{5,3},{3,1},{1,0},{8,10},{10,12},{12... | collective-permute-start | bytes 1572872 | tf_op jit(solution)/shard_map/ppermute | solution.py:106
  31.2 39.6 %all-to-all-start.1 = ((bf16[4,128,1408]{2,1,0:T(8,128)(2,1)}), bf16[4,128,1408]{2,1,0:T(8,128)(2,1)}, u32[]{:S(2)}, u32[]{:S(2)}) async-start(bf16[4,128,1408]{2,1,0:T(8,128)(2,1)} %bitcast.20), calls=%async_computation.1 | async-start | bytes 2883584 | tf_op jit(solution)/shard_map/all_to_all | solution.py:151
  67.3 35.4 %collective-permute-start.3 = (bf16[128,2048]{1,0:T(8,128)(2,1)}, bf16[128,2048]{1,0:T(8,128)(2,1)}, u32[]{:S(2)}, u32[]{:S(2)}) collective-permute-start(bf16[128,2048]{1,0:T(8,128)(2,1)} %collective-permute-done.1), channel_id=1, source_target_pairs={{0,1},{2,0},{4,2},{6,4},{7,6},{5,7},{3,5},{1,3},{8,9},{10,8},{12,1... | collective-permute-start | bytes 1572872 | tf_op jit(solution)/shard_map/ppermute | solution.py:106
  67.9 34.9 %collective-permute-start.2 = (bf16[128,2048]{1,0:T(8,128)(2,1)}, bf16[128,2048]{1,0:T(8,128)(2,1)}, u32[]{:S(2)}, u32[]{:S(2)}) collective-permute-start(bf16[128,2048]{1,0:T(8,128)(2,1)} %collective-permute-done), channel_id=1, source_target_pairs={{0,2},{2,4},{4,6},{6,7},{7,5},{5,3},{3,1},{1,0},{8,10},{10,12},{12... | collective-permute-start | bytes 1572872 | tf_op jit(solution)/shard_map/ppermute | solution.py:106
  70.8 47.7 %all-to-all-start = ((bf16[8,64,768]{2,1,0:T(8,128)(2,1)}), bf16[8,64,768]{2,1,0:T(8,128)(2,1)S(1)}, u32[]{:S(2)}, u32[]{:S(2)}) async-start(bf16[8,64,768]{2,1,0:T(8,128)(2,1)} %reshape.555), calls=%async_computation | async-start | bytes 1572864 | tf_op jit(solution)/shard_map/all_to_all | solution.py:151
  74.9 216.9 %all-gather.6.cloned.1.call-start = ((), (), s32[]{:S(2)}) async-start(), calls=%async_computation.19 | async-start | bytes 4718592 | tf_op jit(solution)/shard_map/all_gather | solution.py:329
  175.7 80.1 %all-to-all-start.4 = ((bf16[8,528,256]{2,1,0:T(8,128)(2,1)}), bf16[8,528,256]{2,1,0:T(8,128)(2,1)S(1)}, u32[]{:S(2)}, u32[]{:S(2)}) async-start(bf16[8,528,256]{2,1,0:T(8,128)(2,1)} %get-tuple-element.47), calls=%async_computation.4 | async-start | bytes 4325376 | tf_op jit(solution)/shard_map/all_to_all | solution.py:151
  272.7 99.9 %all-to-all-start.5 = ((bf16[8,528,256]{2,1,0:T(8,128)(2,1)}), bf16[8,528,256]{2,1,0:T(8,128)(2,1)S(1)}, u32[]{:S(2)}, u32[]{:S(2)}) async-start(bf16[8,528,256]{2,1,0:T(8,128)(2,1)} %get-tuple-element.50), calls=%async_computation.5 | async-start | bytes 4325376 | tf_op jit(solution)/shard_map/all_to_all | solution.py:151
  290.1 41.6 %collective-permute-start.13 = (bf16[128,2048]{1,0:T(8,128)(2,1)}, bf16[128,2048]{1,0:T(8,128)(2,1)}, u32[]{:S(2)}, u32[]{:S(2)}) collective-permute-start(bf16[128,2048]{1,0:T(8,128)(2,1)} %collective-permute-done.11), channel_id=1, source_target_pairs={{0,2},{2,4},{4,6},{6,7},{7,5},{5,3},{3,1},{1,0},{8,10},{10,12},{12... | collective-permute-start | bytes 1572872 | tf_op jit(solution)/shard_map/ppermute | solution.py:106
  291.8 97.7 %collective-permute-start.24 = (bf16[1024,2048]{1,0:T(8,128)(2,1)}, bf16[1024,2048]{1,0:T(8,128)(2,1)}, u32[]{:S(2)}, u32[]{:S(2)}) collective-permute-start(bf16[1024,2048]{1,0:T(8,128)(2,1)} %all-gather.6.cloned.1.call-done), channel_id=1, source_target_pairs={{0,8},{8,0},{16,24},{24,16},{1,9},{9,1},{17,25},{25,17},{2,10},{10... | collective-permute-start | bytes 12582920 | tf_op jit(solution)/shard_map/ppermute | solution.py:155
  324.5 37.7 %collective-permute-start.16 = (bf16[128,2048]{1,0:T(8,128)(2,1)}, bf16[128,2048]{1,0:T(8,128)(2,1)S(1)}, u32[]{:S(2)}, u32[]{:S(2)}) collective-permute-start(bf16[128,2048]{1,0:T(8,128)(2,1)} %collective-permute-done.14), channel_id=1, source_target_pairs={{0,1},{2,0},{4,2},{6,4},{7,6},{5,7},{3,5},{1,3},{8,9},{10,8},{12,1... | collective-permute-start | bytes 1572872 | tf_op jit(solution)/shard_map/ppermute | solution.py:106
  370.1 44.9 %collective-permute-start.19 = (bf16[1024,2048]{1,0:T(8,128)(2,1)}, bf16[1024,2048]{1,0:T(8,128)(2,1)}, u32[]{:S(2)}, u32[]{:S(2)}) collective-permute-start(bf16[1024,2048]{1,0:T(8,128)(2,1)} %constant_dynamic-update-slice_fusion.5), channel_id=1, source_target_pairs={{0,8},{8,0},{16,24},{24,16},{1,9},{9,1},{17,25},{25,17},{2,10},{10... | collective-permute-start | bytes 12582920 | tf_op jit(solution)/shard_map/ppermute | solution.py:155
  372.6 38.7 %all-to-all-start.6 = ((bf16[8,352,256]{2,1,0:T(8,128)(2,1)}), bf16[8,352,256]{2,1,0:T(8,128)(2,1)}, u32[]{:S(2)}, u32[]{:S(2)}) async-start(bf16[8,352,256]{2,1,0:T(8,128)(2,1)} %bitcast.327), calls=%async_computation.6 | async-start | bytes 2883584 | tf_op jit(solution)/shard_map/all_to_all | solution.py:151
  381.9 49.0 %collective-permute-start.21 = (bf16[528,2048]{1,0:T(8,128)(2,1)}, bf16[528,2048]{1,0:T(8,128)(2,1)}, u32[]{:S(2)}, u32[]{:S(2)}) collective-permute-start(bf16[528,2048]{1,0:T(8,128)(2,1)} %pad_maximum_fusion.6), channel_id=1, source_target_pairs={{0,16},{8,24},{16,0},{24,8},{1,17},{9,25},{17,1},{25,9},{2,18},{10... | collective-permute-start | bytes 6488072 | tf_op jit(solution)/shard_map/ppermute | solution.py:160
  385.5 91.8 %collective-permute-start.20 = (bf16[528,2048]{1,0:T(8,128)(2,1)}, bf16[528,2048]{1,0:T(8,128)(2,1)}, u32[]{:S(2)}, u32[]{:S(2)}) collective-permute-start(bf16[528,2048]{1,0:T(8,128)(2,1)} %pad_maximum_fusion.7), channel_id=1, source_target_pairs={{0,16},{8,24},{16,0},{24,8},{1,17},{9,25},{17,1},{25,9},{2,18},{10... | collective-permute-start | bytes 6488072 | tf_op jit(solution)/shard_map/ppermute | solution.py:160
  414.4 109.1 %collective-permute-start.22 = (bf16[528,2048]{1,0:T(8,128)(2,1)}, bf16[528,2048]{1,0:T(8,128)(2,1)}, u32[]{:S(2)}, u32[]{:S(2)}) collective-permute-start(bf16[528,2048]{1,0:T(8,128)(2,1)} %pad_maximum_fusion.8), channel_id=1, source_target_pairs={{0,16},{8,24},{16,0},{24,8},{1,17},{9,25},{17,1},{25,9},{2,18},{10... | collective-permute-start | bytes 6488072 | tf_op jit(solution)/shard_map/ppermute | solution.py:160
  532.7 147.1 %collective-permute-start.23 = (bf16[1024,2048]{1,0:T(8,128)(2,1)}, bf16[1024,2048]{1,0:T(8,128)(2,1)}, u32[]{:S(2)}, u32[]{:S(2)}) collective-permute-start(bf16[1024,2048]{1,0:T(8,128)(2,1)} %convolution_convert_fusion.4), channel_id=1, source_target_pairs={{0,8},{8,0},{16,24},{24,16},{1,9},{9,1},{17,25},{25,17},{2,10},{10... | collective-permute-start | bytes 12582920 | tf_op jit(solution)/shard_map/ppermute | solution.py:155
  566.1 55.7 %collective-permute-start.34 = (f32[12,1024]{1,0:T(8,128)S(1)}, f32[12,1024]{1,0:T(8,128)S(1)}, u32[]{:S(2)}, u32[]{:S(2)}) collective-permute-start(f32[12,1024]{1,0:T(8,128)S(1)} %slice.469), channel_id=1, source_target_pairs={{0,8},{8,0},{16,24},{24,16},{1,9},{9,1},{17,25},{25,17},{2,10},{10... | collective-permute-start | bytes 147464 | tf_op jit(solution)/shard_map/ppermute | solution.py:155
  566.2 98.1 %collective-permute-start.41 = (bf16[528,2048]{1,0:T(8,128)(2,1)}, bf16[528,2048]{1,0:T(8,128)(2,1)}, u32[]{:S(2)}, u32[]{:S(2)}) collective-permute-start(bf16[528,2048]{1,0:T(8,128)(2,1)} %slice.483), channel_id=1, source_target_pairs={{0,16},{8,24},{16,0},{24,8},{1,17},{9,25},{17,1},{25,9},{2,18},{10... | collective-permute-start | bytes 6488072 | tf_op jit(solution)/shard_map/ppermute | solution.py:160
  580.3 141.7 %collective-permute-start.44 = (bf16[528,2048]{1,0:T(8,128)(2,1)}, bf16[528,2048]{1,0:T(8,128)(2,1)}, u32[]{:S(2)}, u32[]{:S(2)}) collective-permute-start(bf16[528,2048]{1,0:T(8,128)(2,1)} %slice.486), channel_id=1, source_target_pairs={{0,16},{8,24},{16,0},{24,8},{1,17},{9,25},{17,1},{25,9},{2,18},{10... | collective-permute-start | bytes 6488072 | tf_op jit(solution)/shard_map/ppermute | solution.py:160
  597.8 41.2 %collective-permute-start.25 = (bf16[1024,2048]{1,0:T(8,128)(2,1)}, bf16[1024,2048]{1,0:T(8,128)(2,1)}, u32[]{:S(2)}, u32[]{:S(2)}) collective-permute-start(bf16[1024,2048]{1,0:T(8,128)(2,1)} %add_convert_fusion.1), channel_id=1, source_target_pairs={{0,8},{8,0},{16,24},{24,16},{1,9},{9,1},{17,25},{25,17},{2,10},{10... | collective-permute-start | bytes 12582920 | tf_op jit(solution)/shard_map/ppermute | solution.py:155
  670.1 66.3 %all-to-all-start.9 = ((bf16[8,352,256]{2,1,0:T(8,128)(2,1)}), bf16[8,352,256]{2,1,0:T(8,128)(2,1)S(1)}, u32[]{:S(2)}, u32[]{:S(2)}) async-start(bf16[8,352,256]{2,1,0:T(8,128)(2,1)} %bitcast.342), calls=%async_computation.10 | async-start | bytes 2883584 | tf_op jit(solution)/shard_map/all_to_all | solution.py:151
  736.4 73.2 %all-to-all-start.10 = ((bf16[8,528,256]{2,1,0:T(8,128)(2,1)}), bf16[8,528,256]{2,1,0:T(8,128)(2,1)}, u32[]{:S(2)}, u32[]{:S(2)}) async-start(bf16[8,528,256]{2,1,0:T(8,128)(2,1)} %pad_maximum_fusion.9), calls=%async_computation.11 | async-start | bytes 4325376 | tf_op jit(solution)/shard_map/all_to_all | solution.py:151
  742.7 309.7 %all-gather.8.cloned.1.call-start = ((), (), s32[]{:S(2)}) async-start(), calls=%async_computation.20 | async-start | bytes 4718592 | tf_op jit(solution)/shard_map/all_gather | solution.py:432
  748.0 46.8 %collective-permute-start.50 = (bf16[528,2048]{1,0:T(8,128)(2,1)S(1)}, bf16[528,2048]{1,0:T(8,128)(2,1)S(1)}, u32[]{:S(2)}, u32[]{:S(2)}) collective-permute-start(bf16[528,2048]{1,0:T(8,128)(2,1)S(1)} %slice.501), channel_id=1, source_target_pairs={{0,16},{8,24},{16,0},{24,8},{1,17},{9,25},{17,1},{25,9},{2,18},{10... | collective-permute-start | bytes 6488072 | tf_op jit(solution)/shard_map/ppermute | solution.py:160
  809.6 79.7 %all-to-all-start.14 = ((bf16[8,528,256]{2,1,0:T(8,128)(2,1)}), bf16[8,528,256]{2,1,0:T(8,128)(2,1)}, u32[]{:S(2)}, u32[]{:S(2)}) async-start(bf16[8,528,256]{2,1,0:T(8,128)(2,1)} %pad_maximum_fusion.10), calls=%async_computation.15 | async-start | bytes 4325376 | tf_op jit(solution)/shard_map/all_to_all | solution.py:151
  893.4 198.9 %reduce-scatter.2.cloned.1.call-start = ((), (), s32[]{:S(2)}) async-start(), calls=%async_computation.18 | async-start | bytes 4718592 | tf_op jit(solution)/shard_map/reduce_scatter | solution.py:394
  918.9 67.0 %all-to-all-start.15 = ((bf16[4,128,1408]{2,1,0:T(8,128)(2,1)}), bf16[4,128,1408]{2,1,0:T(8,128)(2,1)S(1)}, u32[]{:S(2)}, u32[]{:S(2)}) async-start(bf16[4,128,1408]{2,1,0:T(8,128)(2,1)} %bitcast.115), calls=%async_computation.16 | async-start | bytes 2883584 | tf_op jit(solution)/shard_map/all_to_all | solution.py:151
  978.7 41.3 %collective-permute-start.45 = (bf16[2,512,768]{2,1,0:T(8,128)(2,1)}, bf16[2,512,768]{2,1,0:T(8,128)(2,1)}, u32[]{:S(2)}, u32[]{:S(2)}) collective-permute-start(bf16[2,512,768]{2,1,0:T(8,128)(2,1)} %fusion.21), channel_id=1, source_target_pairs={{0,8},{8,0},{16,24},{24,16},{1,9},{9,1},{17,25},{25,17},{2,10},{10... | collective-permute-start | bytes 4718600 | tf_op jit(solution)/shard_map/ppermute | solution.py:155
  979.6 36.9 %collective-permute-start.37 = (bf16[128,2048]{1,0:T(8,128)(2,1)}, bf16[128,2048]{1,0:T(8,128)(2,1)}, u32[]{:S(2)}, u32[]{:S(2)}) collective-permute-start(bf16[128,2048]{1,0:T(8,128)(2,1)} %pad_maximum_fusion.17), channel_id=1, source_target_pairs={{0,2},{2,4},{4,6},{6,7},{7,5},{5,3},{3,1},{1,0},{8,10},{10,12},{12... | collective-permute-start | bytes 1572872 | tf_op jit(solution)/shard_map/ppermute | solution.py:127
  (127 other events, 2587.6 us)
Sparse Core Ops, SparseCore 0:
  11.6 96.2 all-gather.3
  175.8 108.5 all-gather.5
  746.3 134.4 all-gather.7
  897.6 101.0 reduce-scatter.1
where the time goes:
time: 1130 us; the launch traced here: 1120 us
  waiting for transfers between devices  403 us (36%)
  matrix products  226 us (20%)
  starting transfers between devices  175 us (15%)
  local copies, waits for them, and re-layouts  158 us (14%)
  other arithmetic  112 us (10%)
  between operations  28.2 us (2%)
  blocking collectives  16.9 us (1%)
    dot_general x35, matrix products, dot(): lax.dot_general(left, right, (((left_dim,), (right_dim,)), ((), ())), pre...  226 us
    all_to_all x15, waiting for transfers between devices, swap_blocks(): return lax.all_to_all(blocks, axis, split_axis=0, concat_axis=0, tiled=True)  167 us
    ppermute x9, waiting for transfers between devices, along_y(): lax.ppermute(value, E, [(e, (e + 2 * by) % size) for e in range(size)])  104 us
    all_to_all x15, starting transfers between devices, swap_blocks(): return lax.all_to_all(blocks, axis, split_axis=0, concat_axis=0, tiled=True)  80.2 us
    ppermute x12, waiting for transfers between devices, ring_gather(): up, down = (lax.ppermute(up, F, right), lax.ppermute(down, F, left))  63.6 us
    ppermute x16, waiting for transfers between devices, ring_scatter(): up, down = (lax.ppermute(up, F, right), lax.ppermute(down, F, left))  45.1 us
    ppermute x12, starting transfers between devices, ring_gather(): up, down = (lax.ppermute(up, F, right), lax.ppermute(down, F, left))  35.2 us
    unnamed x203, local copies, waits for them, and re-layouts  32.5 us
  transfers between devices with their start and end apart: 70, of which 27 were waited for; matrix products, arithmetic and copies ran while one was open for 42% of the time, Pallas kernels for 0%

commit v1 on v0

--- a/solution.py
+++ b/solution.py
@@ -86,8 +86,8 @@
     return jnp.array(order, jnp.int32)[(at + by) % size]
 
 
-def ring_gather(shard, ties=None):
-    ties = ties or {}
+def ring_gather(shard, work=None):
+    work = work or {}
     size = lax.axis_size(F)
     right, left = ring_shift(size, 1), ring_shift(size, -1)
     rows = shard.shape[0]
@@ -102,11 +102,13 @@
     up = down = shard
     whole = put(whole, shard, 0)
     for step in range(1, size // 2):
-        up, down = tied(up, down, ties.get(step))
+        done = work[step](up) if step in work else None
         up, down = lax.ppermute(up, F, right), lax.ppermute(down, F, left)
+        up, down = tied(up, down, done)
         whole = put(put(whole, up, -step), down, step)
-    up, down = tied(up, down, ties.get(size // 2))
+    done = work[size // 2](up) if size // 2 in work else None
     up, down = lax.ppermute(up[:cut], F, right), lax.ppermute(down[cut:], F, left)
+    up, down = tied(up, down, done)
     return put(put(whole, up, size // 2), down, size // 2, cut)
 
 
@@ -247,22 +249,19 @@
 
     w_out = lax.all_gather(w_output.astype(bf16), EF, axis=0, tiled=True)
     qkv_own = jnp.stack([w_query, w_key, w_value]).astype(bf16).reshape(3, part, n_f, slab)
-    qkv_own = swap_blocks(qkv_own.transpose(2, 1, 0, 3).reshape(n_f, part, 3 * slab), F)
+    qkv_sent = qkv_own.transpose(2, 1, 0, 3).reshape(n_f, part, 3 * slab)
+    qkv_own = swap_blocks(qkv_sent, F)
     w_qkv = gather_e(qkv_own.reshape(n_f * part, 3 * slab))
 
-    def by_hidden(expert_weight, shared_weight):
+    def routed_blocks(expert_weight):
         routed = expert_weight.astype(bf16).transpose(0, 2, 1).reshape(own, n_f, per_expert, slab)
-        routed = routed.transpose(1, 0, 2, 3).reshape(n_f, own * per_expert, slab)
-        shared = shared_weight.T.reshape(n_f, per_shared, slab)
-        return jnp.concatenate([routed, shared], axis=1)
-
-    shared_two = jnp.stack([shared_wgate, shared_wup]).astype(bf16)
-    shared_two = shared_two.reshape(2, part, n_e, n_f * per_shared).transpose(2, 0, 1, 3)
-    shared_two = swap_blocks(shared_two.reshape(n_e, 2 * part, n_f * per_shared), E)
-    shared_two = shared_two.reshape(n_e, 2, part, n_f * per_shared).transpose(1, 0, 2, 3)
-    shared_two = shared_two.reshape(2, n_e * part, n_f * per_shared)
-    gate_blocks = by_hidden(expert_wgate, shared_two[0])
-    up_blocks = by_hidden(expert_wup, shared_two[1])
+        return routed.transpose(1, 0, 2, 3).reshape(n_f, own * per_expert, slab)
+
+    def shared_slabs(anchor):
+        two = jnp.stack([after(shared_wgate, anchor), shared_wup]).astype(bf16)
+        two = two.reshape(2, part, n_e, n_f * per_shared).transpose(2, 0, 1, 3)
+        return two.reshape(n_e, 2 * part, n_f * per_shared)
+
     routed_down = expert_wdown.astype(bf16).reshape(own, n_f, per_expert, slab)
     routed_down = routed_down.transpose(1, 0, 2, 3).reshape(n_f, own * per_expert, slab)
 
@@ -276,17 +275,41 @@
         return jnp.concatenate([routed, shared])
 
     def both_levels(mine):
-        return jnp.concatenate([mine] + [along_y(mine, by) for by in range(1, levels)])
+        return lax.all_gather(mine, E, axis=0, tiled=True, axis_index_groups=along_levels)
 
     levels = n_e // 2
-    x_all = ring_gather(tokens, {n_f // 2: (qkv_own, gate_blocks, up_blocks, routed_down)})
-    gate_mine = swap_blocks(after(gate_blocks, x_all), F)
-    up_mine = swap_blocks(after(up_blocks, x_all), F)
+    along_levels = [[2 * level + core for level in range(levels)] for core in range(2)]
+    made = {}
+
+    def work_one(sent):
+        made["shared"] = shared_slabs(sent)
+        return made["shared"], qkv_sent
+
+    def work_two(sent):
+        made["gate"] = routed_blocks(after(expert_wgate, sent))
+        made["up"] = routed_blocks(after(expert_wup, sent))
+        return made["gate"], made["up"]
+
+    def work_three(sent):
+        two = swap_blocks(made["shared"], E).reshape(n_e, 2, part, n_f * per_shared)
+        two = after(two, sent).transpose(1, 3, 0, 2)
+        made["two"] = two.reshape(2, n_f, per_shared, slab)
+        return made["two"], qkv_own
+
+    def work_four(sent):
+        gate, up = after((made["gate"], made["up"]), sent)
+        made["both"] = jnp.concatenate([gate, made["two"][0], up, made["two"][1]], axis=1)
+        return made["both"], routed_down
+
+    x_all = ring_gather(
+        tokens, {1: work_one, 2: work_two, n_f // 2 - 1: work_three, n_f // 2: work_four}
+    )
+    both_raw = swap_blocks(after(made["both"], x_all), F)
+    g_all = lax.all_gather(after(cotangent, qkv_own), F, axis=0, tiled=True)
 
     blocks = own + 1
     column = jnp.arange(levels * hidden_own, dtype=jnp.int32)
-    level_of = (at_e // 2 - column // hidden_own) % levels
-    block_of = (2 * level_of + at_e % 2) * blocks + jnp.minimum(
+    block_of = (2 * (column // hidden_own) + at_e % 2) * blocks + jnp.minimum(
         (column % hidden_own) // per_expert, own
     )
     spread = (jnp.arange(n_e * blocks, dtype=jnp.int32)[:, None] == block_of[None, :]).astype(f32)
@@ -317,23 +340,26 @@
         mixed_parts.append(product(probs.astype(bf16), v).astype(bf16))
         saved.append((q, k, v, probs))
     mixed = jnp.concatenate(mixed_parts, axis=1)
-    gate_mine = gate_like(after(gate_mine, mixed))
-    w_gate = both_levels(gate_mine)
+    mixed = after(mixed, both_raw)
     mixed_own = swap_blocks(mixed.reshape(n_f, rows, slab), F)
-    up_mine = gate_like(after(up_mine, mixed_own))
+    down_raw = swap_blocks(after(routed_down, mixed_own), F)
+    gate_mine = gate_like(both_raw[:, :hidden_own])
+    mixed_own = after(mixed_own, gate_mine)
     mixed_own = mixed_own.transpose(1, 0, 2).reshape(rows, width)
     hidden = tokens.astype(f32) + product(mixed_own, w_out)
 
     ffn_own = (hidden * inverse_rms(hidden) * gain_two).astype(bf16)
-    w_up = both_levels(up_mine)
-    g_all = lax.all_gather(after(cotangent, mixed_own), F, axis=0, tiled=True)
+    def work_ffn(sent):
+        made["up"] = gate_like(after(both_raw, sent)[:, hidden_own:])
+        return made["up"]
+
+    w_gate = both_levels(gate_mine)
+    ffn_all = ring_gather(ffn_own, {1: work_ffn, n_f // 2 - 1: lambda sent: down_raw})
+    w_up = both_levels(made["up"])
+    down_mine = jnp.concatenate([full_width(down_raw), shared_wdown.astype(bf16)])
+    w_down = both_levels(down_mine)
+    ffn_both = jnp.concatenate([ffn_all, sibling(ffn_all)])
     g_both = jnp.concatenate([g_all, sibling(g_all)])
-    down_mine = swap_blocks(after(routed_down, mixed_own), F)
-    ffn_all = ring_gather(after(ffn_own, up_mine))
-    ffn_both = jnp.concatenate([ffn_all, sibling(ffn_all)])
-    down_mine = full_width(after(down_mine, ffn_all))
-    down_mine = jnp.concatenate([down_mine, shared_wdown.astype(bf16)])
-    w_down = both_levels(down_mine)
 
     named = jnp.arange(experts, dtype=jnp.int32).astype(bf16)
     ids = jnp.concatenate([ids_of(at_e), ids_of(at_e ^ 1)])
@@ -359,14 +385,26 @@
     mid_scaled = (mid * scale).astype(bf16)
 
     def over_levels(grad):
-        total = grad[:hidden_own].astype(f32)
-        for by in range(1, levels):
-            there = grad[by * hidden_own : (by + 1) * hidden_own]
-            total = total + along_y(there, -by).astype(f32)
-        return total.astype(bf16)
-
-    d_down_all = contract(mid_scaled, after(g_both, down_mine)).astype(bf16)
-    d_down = over_levels(d_down_all)
+        return lax.psum_scatter(
+            grad, E, scatter_dimension=0, tiled=True, axis_index_groups=along_levels
+        )
+
+    d_down_all = contract(mid_scaled, g_both).astype(bf16)
+    def by_slab(grad):
+        return grad.reshape(grad.shape[0], n_f, slab).transpose(1, 0, 2)
+
+    def gate_slabs(grad):
+        routed, shared = grad[: own * per_expert], grad[own * per_expert :]
+        shared = shared.reshape(per_shared, n_e, n_f, part).transpose(2, 0, 1, 3)
+        shared = shared.reshape(n_f, per_shared, slab)
+        return jnp.concatenate([by_slab(routed), shared], axis=1)
+
+    def return_routed(back):
+        back = back.reshape(n_f, own, per_expert, slab).transpose(1, 0, 2, 3)
+        return back.reshape(own, n_f * per_expert, slab)
+
+    def return_gate(back):
+        return return_routed(back[:, : own * per_expert]).transpose(0, 2, 1).astype(f32)
 
     mid_grad = product_t(after(g_both, d_down_all), w_down)
     sums = dot(spread, mid * mid_grad, 1, 1, highest)
@@ -374,25 +412,29 @@
     gate_grad = (scaled * pre_up * slope).astype(bf16)
     up_grad = (scaled * silu).astype(bf16)
 
+    d_down = over_levels(d_down_all)
+    d_gate_all = contract(gate_grad, ffn_both).astype(bf16)
+    d_up_all = contract(up_grad, ffn_both).astype(bf16)
+    gate_grad, up_grad = lax.optimization_barrier((gate_grad, up_grad, d_gate_all, d_up_all))[:2]
+
     def input_grad(first):
         rows_of = slice(first, first + seq)
         return product(gate_grad[rows_of], w_gate) + product(up_grad[rows_of], w_up)
 
     from_sibling = sibling(input_grad(seq).astype(bf16))
-    moe_sibling = sibling(product(mid_scaled[seq:], w_down).astype(bf16))
     gate_sums = sums[:, :seq] + sibling(sums[:, seq:])
     gate_sums = gate_sums.reshape(n_e * blocks, n_f, rows).transpose(1, 0, 2)
+    terms = (input_grad(0) + from_sibling.astype(f32)).astype(bf16)
     gate_sums = jnp.sum(swap_blocks(gate_sums, F), axis=0)
-    d_gate_all = contract(gate_grad, ffn_both).astype(bf16)
-    d_up_all = contract(up_grad, ffn_both).astype(bf16)
+    d_down = after(d_down, terms)
+    d_down_back = swap_blocks(after(by_slab(d_down[: own * per_expert]), gate_sums), F)
     d_gate, d_up = over_levels(d_gate_all), over_levels(d_up_all)
+    moe_sibling = sibling(product(after(mid_scaled, terms)[seq:], w_down).astype(bf16))
     moe = (product(mid_scaled[:seq], w_down) + moe_sibling.astype(f32)).astype(bf16)
+    d_expert_down = return_routed(d_down_back).astype(f32)
     ffn_grad = ring_scatter(
-        (input_grad(0) + from_sibling.astype(f32)).astype(bf16),
-        {3: d_gate_all, 2: d_up_all, 1: moe, 0: gate_sums},
-    )
-    moe = lax.psum_scatter(moe, F, scatter_dimension=0, tiled=True)
-    output = (hidden + moe.astype(f32)).astype(bf16)
+        terms, {3: (gate_sums, moe_sibling), 2: moe, 1: d_expert_down}
+    )
     gate_sums = gate_sums.T.reshape(rows, n_e, blocks)
 
     def mine(table):
@@ -413,23 +455,15 @@
     d_gain_two = jnp.sum(ffn_grad * hidden_hat, axis=0)
     hidden_grad = cotangent.astype(f32) + hidden_back
 
-    def by_slab(grad):
-        return grad.reshape(grad.shape[0], n_f, slab).transpose(1, 0, 2)
-
-    def gate_slabs(grad):
-        routed, shared = grad[: own * per_expert], grad[own * per_expert :]
-        shared = shared.reshape(per_shared, n_e, n_f, part).transpose(2, 0, 1, 3)
-        shared = shared.reshape(n_f, per_shared, slab)
-        return jnp.concatenate([by_slab(routed), shared], axis=1)
-
     hidden_low = hidden_grad.astype(bf16)
     mixed_grad = product_t(hidden_low, w_out).astype(bf16).reshape(rows, n_f, slab)
     mixed_grad = swap_blocks(mixed_grad.transpose(1, 0, 2), F)
-    d_down_back = swap_blocks(by_slab(d_down[: own * per_expert]), F)
-    gate_back = swap_blocks(gate_slabs(d_gate), F)
-    up_back = swap_blocks(gate_slabs(d_up), F)
+    gate_back = swap_blocks(after(gate_slabs(d_gate), mixed_grad), F)
+    up_back = swap_blocks(after(gate_slabs(d_up), gate_back), F)
     mixed_grad = mixed_grad.reshape(seq, slab)
-    hidden_low = lax.all_gather(hidden_low, F, axis=0, tiled=True)
+    hidden_low = lax.all_gather(after(hidden_low, d_up), F, axis=0, tiled=True)
+    moe = lax.psum_scatter(after(moe, hidden_low), F, scatter_dimension=0, tiled=True)
+    output = (hidden + moe.astype(f32)).astype(bf16)
     d_out = contract(mixed, hidden_low)
     lin_grads = [[], [], []]
     for h in range(heads):
@@ -446,22 +480,14 @@
     lin_grad = jnp.concatenate(lin_grads[0] + lin_grads[1] + lin_grads[2], axis=1)
     normed_part = product_t(lin_grad, w_qkv).astype(bf16)
     d_qkv = contract(normed, lin_grad)
-    normed_grad = ring_scatter(normed_part, {3: d_qkv, 1: d_down_back, 0: gate_back})
+    d_expert_gate, d_expert_up = return_gate(gate_back), return_gate(up_back)
+    normed_grad = ring_scatter(normed_part, {3: d_qkv, 2: d_expert_gate, 0: up_back})
     d_bias = jnp.sum(lin_grad.astype(f32), axis=0).reshape(3, slab)
     d_gain_one = jnp.sum(d_qkv * w_qkv.astype(f32), axis=1) / gain_one
     token_back, unused = norm_back(tokens.astype(f32), gain_one, normed_grad)
     token_grad = (hidden_grad + token_back).astype(bf16)
 
-    def return_routed(back):
-        back = back.reshape(n_f, own, per_expert, slab).transpose(1, 0, 2, 3)
-        return back.reshape(own, n_f * per_expert, slab)
-
-    def return_gate(back):
-        return return_routed(back[:, : own * per_expert]).transpose(0, 2, 1).astype(f32)
-
     d_shared_down = d_down[own * per_expert :].astype(f32)
-    d_expert_down = return_routed(d_down_back).astype(f32)
-    d_expert_gate, d_expert_up = return_gate(gate_back), return_gate(up_back)
     shared_two = jnp.stack([gate_back[:, own * per_expert :], up_back[:, own * per_expert :]])
     shared_two = shared_two.reshape(2, n_f * per_shared, slab).transpose(0, 2, 1)
     shared_two = shared_two.reshape(2, n_e, part, n_f * per_shared).transpose(1, 0, 2, 3)
@@ -481,9 +507,8 @@
         jnp.zeros((3, width), f32), d_bias, at_f * slab, 1
     )
     d_small = jnp.concatenate([bias_rows, d_gain_one[None], d_gain_two[None], d_route])
-    d_small = d_small.reshape(6 + experts, n_e, n_f, part).transpose(2, 1, 0, 3)
-    d_small = jnp.sum(swap_blocks(d_small, F), axis=0)
-    d_small = jnp.sum(swap_blocks(d_small, E), axis=0)
+    d_small = d_small.reshape(6 + experts, devices, part).transpose(1, 0, 2)
+    d_small = jnp.sum(swap_blocks(d_small, EF), axis=0)
 
     return (
         output,

time: 1130 us -> 1070 us (0.947)
  other arithmetic: 112 us -> 72.1 us
  waiting for transfers between devices: 403 us -> 374 us
  blocking collectives: 16.9 us -> 0 us
  local copies, waits for them, and re-layouts: 158 us -> 172 us
    ppermute x9 -> x3, waiting for transfers between devices: 104 us -> 29.2 us  [along_y(): lax.ppermute(value, E, [(e, (e + 2 * by) % size) for e in range(size)])]
    ppermute x16, waiting for transfers between devices: 45.1 us -> 103 us  [ring_scatter(): up, down = (lax.ppermute(up, F, right), lax.ppermute(down, F, left))]
    ppermute x12, waiting for transfers between devices: 63.6 us -> 38.7 us  [ring_gather(): up, down = (lax.ppermute(up, F, right), lax.ppermute(down, F, left))]
    convert_element_type x6 -> x2, other arithmetic: 22.6 us -> 1.74 us  [the longest x1 1.45 us: shards(): shared_wdown.astype(bf16)]
    all_to_all x1 -> x0, blocking collectives: 16.9 us -> none  [swap_blocks(): return lax.all_to_all(blocks, axis, split_axis=0, concat_axis=0, tiled=True)]
    all_to_all x15 -> x14, waiting for transfers between devices: 167 us -> 183 us  [swap_blocks(): return lax.all_to_all(blocks, axis, split_axis=0, concat_axis=0, tiled=True)]
    ppermute x12, starting transfers between devices: 35.2 us -> 21.2 us  [ring_gather(): up, down = (lax.ppermute(up, F, right), lax.ppermute(down, F, left))]
    ppermute x16, starting transfers between devices: 20.9 us -> 33.5 us  [ring_scatter(): up, down = (lax.ppermute(up, F, right), lax.ppermute(down, F, left))]
  transfers between devices with their start and end apart: 70 -> 69, of which waited for: 27 -> 27; matrix products, arithmetic and copies ran while one was open for 42% -> 43% of each run, Pallas kernels for 0% -> 0%
where the time goes in v1:
time: 1070 us; the launch traced here: 1060 us
  waiting for transfers between devices  374 us (35%)
  matrix products  231 us (22%)
  starting transfers between devices  177 us (17%)
  local copies, waits for them, and re-layouts  172 us (16%)
  other arithmetic  72.1 us (7%)
  between operations  28.8 us (3%)
    dot_general x35, matrix products, dot(): lax.dot_general(left, right, (((left_dim,), (right_dim,)), ((), ())), pre...  231 us
    all_to_all x14, waiting for transfers between devices, swap_blocks(): return lax.all_to_all(blocks, axis, split_axis=0, concat_axis=0, tiled=True)  183 us
    ppermute x16, waiting for transfers between devices, ring_scatter(): up, down = (lax.ppermute(up, F, right), lax.ppermute(down, F, left))  103 us
    all_to_all x14, starting transfers between devices, swap_blocks(): return lax.all_to_all(blocks, axis, split_axis=0, concat_axis=0, tiled=True)  92 us
    unnamed x210, local copies, waits for them, and re-layouts  41.8 us
    ppermute x12, waiting for transfers between devices, ring_gather(): up, down = (lax.ppermute(up, F, right), lax.ppermute(down, F, left))  38.7 us
    ppermute x16, starting transfers between devices, ring_scatter(): up, down = (lax.ppermute(up, F, right), lax.ppermute(down, F, left))  33.5 us
    ppermute x3, waiting for transfers between devices, along_y(): lax.ppermute(value, E, [(e, (e + 2 * by) % size) for e in range(size)])  29.2 us
  transfers between devices with their start and end apart: 69, of which 27 were waited for; matrix products, arithmetic and copies ran while one was open for 43% of the time, Pallas kernels for 0%

profile of v1, /device:TPU:1, one launch (start us, length us, event | category | flops | bytes accessed | tf_op | source)
XLA Modules:
  0.0 1055.7 jit_solution(12099318232177227879)
XLA Ops:
  88.2 9.0 all-to-all-done
  97.2 10.1 all-to-all-start.2
  107.4 9.5 collective-permute-done.5
  146.3 11.6 %collective-permute-done.9 = bf16[512,768]{1,0:T(8,128)(2,1)S(1)} collective-permute-done((bf16[512,768]{1,0:T(8,128)(2,1)S(1)}, bf16[512,768]{1,0:T(8,128)(2,1)S(1)}, u32[]{:S(2)}, u32[]{:S(2)}) %collective-permute-start.9) | collective-permute-done | bytes 786464 | tf_op jit(solution)/shard_map/ppermute | solution.py:162
  180.7 101.8 %all-to-all-done.3 = bf16[8,1056,256]{2,1,0:T(8,128)(2,1)} async-done(((bf16[8,1056,256]{2,1,0:T(8,128)(2,1)}), bf16[8,1056,256]{2,1,0:T(8,128)(2,1)}, u32[]{:S(2)}, u32[]{:S(2)}) %all-to-all-start.3) | async-done | bytes 4325408 | tf_op jit(solution)/shard_map/all_to_all | solution.py:153
  301.0 13.4 %all-to-all-done.4 = bf16[8,128,256]{1,2,0:T(8,128)(2,1)S(1)} async-done(((bf16[8,128,256]{1,2,0:T(8,128)(2,1)}), bf16[8,128,256]{1,2,0:T(8,128)(2,1)S(1)}, u32[]{:S(2)}, u32[]{:S(2)}) %all-to-all-start.4) | async-done | bytes 524320 | tf_op jit(solution)/shard_map/all_to_all | solution.py:153
  314.4 15.9 %all-to-all-start.5 = ((bf16[8,352,256]{2,1,0:T(8,128)(2,1)}), bf16[8,352,256]{2,1,0:T(8,128)(2,1)S(1)}, u32[]{:S(2)}, u32[]{:S(2)}) async-start(bf16[8,352,256]{2,1,0:T(8,128)(2,1)} %bitcast.30), calls=%async_computation.5 | async-start | bytes 2883584 | tf_op jit(solution)/shard_map/all_to_all | solution.py:153
  346.4 16.9 %collective-permute-done.11 = bf16[128,2048]{1,0:T(8,128)(2,1)} collective-permute-done((bf16[128,2048]{1,0:T(8,128)(2,1)}, bf16[128,2048]{1,0:T(8,128)(2,1)}, u32[]{:S(2)}, u32[]{:S(2)}) %collective-permute-start.11) | collective-permute-done | bytes 524320 | tf_op jit(solution)/shard_map/ppermute | solution.py:106
  364.8 9.8 collective-permute-start.13
  431.2 15.5 %fusion.132 = f32[2048,1056]{0,1:T(8,128)} fusion(bf16[1056,2048]{1,0:T(8,128)(2,1)} %all-gather.9.cloned.1.call-done, bf16[1024,2048]{1,0:T(8,128)(2,1)} %collective-permute-done.19, bf16[1024,2048]{1,0:T(8,128)(2,1)} %constant_dynamic-update-slice_fusion.5), kind=kOutput, calls=%fused_computation.327 | convolution fusion | flops 8875147264 | bytes 21364736 | tf_op jit(solution)/shard_map/dot_general | solution.py:22
  446.7 16.3 %fusion.131 = f32[2048,1056]{0,1:T(8,128)} fusion(bf16[1056,2048]{1,0:T(8,128)(2,1)} %all-gather.11.cloned.1.call-done, bf16[1024,2048]{1,0:T(8,128)(2,1)} %collective-permute-done.19, bf16[1024,2048]{1,0:T(8,128)(2,1)} %constant_dynamic-update-slice_fusion.5), kind=kOutput, calls=%fused_computation.326 | convolution fusion | flops 8875147264 | bytes 21364736 | tf_op jit(solution)/shard_map/dot_general | solution.py:22
  463.2 12.0 %fusion = (bf16[2048,1056]{0,1:T(8,128)(2,1)S(1)}, bf16[2048,1056]{0,1:T(8,128)(2,1)}, f32[2048,1056]{0,1:T(8,128)}) fusion(f32[2048,1056]{0,1:T(8,128)} %fusion.131, f32[2048,1056]{0,1:T(8,128)} %fusion.132, f32[2048,12]{0,1:T(8,128)S(1)} %reshape.539, s32[1056]{0:T(1024)S(1)} %fusion.100), kind=kOutput, calls=%fused_computation.4 | convolution fusion | flops 330903936 | bytes 34705536 | tf_op jit(solution)/shard_map/dot_general | solution.py:22
  477.1 13.3 %convolution_convert_fusion.2 = bf16[1056,2048]{1,0:T(8,128)(2,1)} fusion(bf16[2048,1056]{0,1:T(8,128)(2,1)S(1)} %get-tuple-element.92, bf16[2048,2048]{1,0:T(8,128)(2,1)} %constant_dynamic-update-slice_fusion), kind=kOutput, calls=%fused_computation.20 | convolution fusion | flops 8860532736 | bytes 17039360 | tf_op jit(solution)/shard_map/dot_general | solution.py:22
  495.2 24.5 %multiply_convert_fusion = (bf16[2048,1056]{0,1:T(8,128)(2,1)}, bf16[2048,1056]{0,1:T(8,128)(2,1)}, f32[2048,1056]{0,1:T(8,128)}) fusion(f32[2048,1056]{0,1:T(8,128)} %get-tuple-element.307, f32[2048,1056]{0,1:T(8,128)} %fusion.132, f32[2048,1056]{0,1:T(8,128)} %fusion.131, bf16[2048,2048]{1,0:T(8,128)(2,1)} %constant_dynamic-update-slice_fusion, ...), kind=kOutput, calls=%fused_computation.6 | convolution fusion | flops 8888647680 | bytes 55967744 | tf_op jit(solution)/shard_map/dot_general | solution.py:22
  519.6 14.3 %convolution_convert_fusion = bf16[1056,2048]{1,0:T(8,128)(2,1)} fusion(bf16[2048,1056]{0,1:T(8,128)(2,1)} %get-tuple-element.91, bf16[1024,2048]{1,0:T(8,128)(2,1)} %collective-permute-done.19, bf16[1024,2048]{1,0:T(8,128)(2,1)} %constant_dynamic-update-slice_fusion.5), kind=kOutput, calls=%fused_computation.18 | convolution fusion | flops 8877309952 | bytes 17039360 | tf_op jit(solution)/shard_map/dot_general | solution.py:22
  533.9 14.4 %convolution_convert_fusion.1 = bf16[1056,2048]{1,0:T(8,128)(2,1)} fusion(bf16[2048,1056]{0,1:T(8,128)(2,1)} %get-tuple-element.90, bf16[1024,2048]{1,0:T(8,128)(2,1)} %collective-permute-done.19, bf16[1024,2048]{1,0:T(8,128)(2,1)} %constant_dynamic-update-slice_fusion.5), kind=kOutput, calls=%fused_computation.19 | convolution fusion | flops 8877309952 | bytes 17039360 | tf_op jit(solution)/shard_map/dot_general | solution.py:22
  548.3 8.6 fusion.18
  556.8 9.8 add_convert_fusion.2
  567.7 8.3 fusion.21
  576.1 10.4 add_convert_fusion.1
  593.7 8.1 fusion.1
  626.3 10.2 add_convert_fusion
  639.7 22.7 %collective-permute-done.28 = bf16[128,2048]{1,0:T(8,128)(2,1)S(1)} collective-permute-done((bf16[128,2048]{1,0:T(8,128)(2,1)S(1)}, bf16[128,2048]{1,0:T(8,128)(2,1)S(1)}, u32[]{:S(2)}, u32[]{:S(2)}) %collective-permute-start.28) | collective-permute-done | bytes 524320 | tf_op jit(solution)/shard_map/ppermute | solution.py:129
  667.7 9.3 collective-permute-start.30
  702.6 7.6 all-to-all-done.8
  724.8 10.0 multiply_reduce_fusion
  738.5 9.1 all-to-all-start.12
  777.7 17.6 %collective-permute-done.41 = bf16[512,768]{1,0:T(8,128)(2,1)} collective-permute-done((bf16[512,768]{1,0:T(8,128)(2,1)S(1)}, bf16[512,768]{1,0:T(8,128)(2,1)}, u32[]{:S(2)}, u32[]{:S(2)}) %collective-permute-start.41) | collective-permute-done | bytes 786464 | tf_op jit(solution)/shard_map/ppermute | solution.py:162
  798.1 45.4 %all-to-all-done.9 = bf16[8,528,256]{2,1,0:T(8,128)(2,1)} async-done(((bf16[8,528,256]{2,1,0:T(8,128)(2,1)}), bf16[8,528,256]{2,1,0:T(8,128)(2,1)}, u32[]{:S(2)}, u32[]{:S(2)}) %all-to-all-start.9) | async-done | bytes 2162720 | tf_op jit(solution)/shard_map/all_to_all | solution.py:153
  866.6 11.6 %collective-permute-done.32 = bf16[64,2048]{1,0:T(8,128)(2,1)} collective-permute-done((bf16[64,2048]{1,0:T(8,128)(2,1)}, bf16[64,2048]{1,0:T(8,128)(2,1)}, u32[]{:S(2)}, u32[]{:S(2)}) %collective-permute-start.32) | collective-permute-done | bytes 262176 | tf_op jit(solution)/shard_map/ppermute | solution.py:129
  896.6 55.2 %collective-permute-done.34 = bf16[128,2048]{1,0:T(8,128)(2,1)} collective-permute-done((bf16[128,2048]{1,0:T(8,128)(2,1)}, bf16[128,2048]{1,0:T(8,128)(2,1)}, u32[]{:S(2)}, u32[]{:S(2)}) %collective-permute-start.34) | collective-permute-done | bytes 524320 | tf_op jit(solution)/shard_map/ppermute | solution.py:129
  958.1 13.9 %collective-permute-start.36 = (bf16[128,2048]{1,0:T(8,128)(2,1)}, bf16[128,2048]{1,0:T(8,128)(2,1)}, u32[]{:S(2)}, u32[]{:S(2)}) collective-permute-start(bf16[128,2048]{1,0:T(8,128)(2,1)} %get-tuple-element.106), channel_id=1, source_target_pairs={{0,2},{2,4},{4,6},{6,7},{7,5},{5,3},{3,1},{1,0},{8,10},{10,12},{12... | collective-permute-start | bytes 1572872 | tf_op jit(solution)/shard_map/ppermute | solution.py:129
  (600 shorter events, 460.8 us)
Async XLA Ops:
  7.2 323.2 %all-gather.7.cloned.1.call-start = ((), (), s32[]{:S(2)}) async-start(), calls=%async_computation.18 | async-start | bytes 8650752 | tf_op jit(solution)/shard_map/all_gather | solution.py:250
  9.0 31.3 %collective-permute-start = (bf16[128,2048]{1,0:T(8,128)(2,1)}, bf16[128,2048]{1,0:T(8,128)(2,1)}, u32[]{:S(2)}, u32[]{:S(2)}) collective-permute-start(bf16[128,2048]{1,0:T(8,128)(2,1)} %param.88), channel_id=1, source_target_pairs={{0,2},{2,4},{4,6},{6,7},{7,5},{5,3},{3,1},{1,0},{8,10},{10,12},{12... | collective-permute-start | bytes 1572872 | tf_op jit(solution)/shard_map/ppermute | solution.py:106
  11.2 29.1 %collective-permute-start.1 = (bf16[128,2048]{1,0:T(8,128)(2,1)}, bf16[128,2048]{1,0:T(8,128)(2,1)}, u32[]{:S(2)}, u32[]{:S(2)}) collective-permute-start(bf16[128,2048]{1,0:T(8,128)(2,1)} %param.88), channel_id=1, source_target_pairs={{0,1},{2,0},{4,2},{6,4},{7,6},{5,7},{3,5},{1,3},{8,9},{10,8},{12,1... | collective-permute-start | bytes 1572872 | tf_op jit(solution)/shard_map/ppermute | solution.py:106
  16.0 45.9 %all-to-all-start.1 = ((bf16[4,128,1408]{2,1,0:T(8,128)(2,1)}), bf16[4,128,1408]{2,1,0:T(8,128)(2,1)S(1)}, u32[]{:S(2)}, u32[]{:S(2)}) async-start(bf16[4,128,1408]{2,1,0:T(8,128)(2,1)} %bitcast.328), calls=%async_computation.1 | async-start | bytes 2883584 | tf_op jit(solution)/shard_map/all_to_all | solution.py:153
  40.3 31.1 %collective-permute-start.2 = (bf16[128,2048]{1,0:T(8,128)(2,1)}, bf16[128,2048]{1,0:T(8,128)(2,1)}, u32[]{:S(2)}, u32[]{:S(2)}) collective-permute-start(bf16[128,2048]{1,0:T(8,128)(2,1)} %collective-permute-done), channel_id=1, source_target_pairs={{0,2},{2,4},{4,6},{6,7},{7,5},{5,3},{3,1},{1,0},{8,10},{10,12},{12... | collective-permute-start | bytes 1572872 | tf_op jit(solution)/shard_map/ppermute | solution.py:106
  42.0 29.4 %collective-permute-start.3 = (bf16[128,2048]{1,0:T(8,128)(2,1)}, bf16[128,2048]{1,0:T(8,128)(2,1)}, u32[]{:S(2)}, u32[]{:S(2)}) collective-permute-start(bf16[128,2048]{1,0:T(8,128)(2,1)} %collective-permute-done.1), channel_id=1, source_target_pairs={{0,1},{2,0},{4,2},{6,4},{7,6},{5,7},{3,5},{1,3},{8,9},{10,8},{12,1... | collective-permute-start | bytes 1572872 | tf_op jit(solution)/shard_map/ppermute | solution.py:106
  61.9 35.3 %all-to-all-start = ((bf16[8,64,768]{2,1,0:T(8,128)(2,1)}), bf16[8,64,768]{2,1,0:T(8,128)(2,1)S(1)}, u32[]{:S(2)}, u32[]{:S(2)}) async-start(bf16[8,64,768]{2,1,0:T(8,128)(2,1)} %reshape.517), calls=%async_computation | async-start | bytes 1572864 | tf_op jit(solution)/shard_map/all_to_all | solution.py:153
  71.4 36.0 %collective-permute-start.4 = (bf16[128,2048]{1,0:T(8,128)(2,1)}, bf16[128,2048]{1,0:T(8,128)(2,1)}, u32[]{:S(2)}, u32[]{:S(2)}) collective-permute-start(bf16[128,2048]{1,0:T(8,128)(2,1)} %collective-permute-done.2), channel_id=1, source_target_pairs={{0,2},{2,4},{4,6},{6,7},{7,5},{5,3},{3,1},{1,0},{8,10},{10,12},{12... | collective-permute-start | bytes 1572872 | tf_op jit(solution)/shard_map/ppermute | solution.py:106
  72.9 44.0 %collective-permute-start.5 = (bf16[128,2048]{1,0:T(8,128)(2,1)}, bf16[128,2048]{1,0:T(8,128)(2,1)}, u32[]{:S(2)}, u32[]{:S(2)}) collective-permute-start(bf16[128,2048]{1,0:T(8,128)(2,1)} %collective-permute-done.3), channel_id=1, source_target_pairs={{0,1},{2,0},{4,2},{6,4},{7,6},{5,7},{3,5},{1,3},{8,9},{10,8},{12,1... | collective-permute-start | bytes 1572872 | tf_op jit(solution)/shard_map/ppermute | solution.py:106
  97.2 36.0 %all-to-all-start.2 = ((bf16[32,2,704]{2,1,0:T(2,128)(2,1)}), bf16[32,2,704]{2,1,0:T(2,128)(2,1)}, u32[]{:S(2)}, u32[]{:S(2)}) async-start(bf16[32,2,704]{2,1,0:T(2,128)(2,1)} %reshape.579), calls=%async_computation.2 | async-start | bytes 196608 | tf_op jit(solution)/shard_map/all_to_all | solution.py:153
  133.2 149.4 %all-to-all-start.3 = ((bf16[8,1056,256]{2,1,0:T(8,128)(2,1)}), bf16[8,1056,256]{2,1,0:T(8,128)(2,1)}, u32[]{:S(2)}, u32[]{:S(2)}) async-start(bf16[8,1056,256]{2,1,0:T(8,128)(2,1)} %pad_maximum_fusion.1), calls=%async_computation.3 | async-start | bytes 8650752 | tf_op jit(solution)/shard_map/all_to_all | solution.py:153
  138.0 236.7 %all-gather.15.cloned.1.call-start = ((), (), s32[]{:S(2)}) async-start(), calls=%async_computation.22 | async-start | bytes 4718592 | tf_op jit(solution)/shard_map/all_gather | solution.py:308
  138.7 292.4 %all-gather.9.cloned.1.call-start = ((), (), s32[]{:S(2)}) async-start(), calls=%async_computation.19 | async-start | bytes 6488064 | tf_op jit(solution)/shard_map/all_gather | solution.py:278
  314.4 78.1 %all-to-all-start.5 = ((bf16[8,352,256]{2,1,0:T(8,128)(2,1)}), bf16[8,352,256]{2,1,0:T(8,128)(2,1)S(1)}, u32[]{:S(2)}, u32[]{:S(2)}) async-start(bf16[8,352,256]{2,1,0:T(8,128)(2,1)} %bitcast.30), calls=%async_computation.5 | async-start | bytes 2883584 | tf_op jit(solution)/shard_map/all_to_all | solution.py:153
  330.3 116.4 %all-gather.11.cloned.1.call-start = ((), (), s32[]{:S(2)}) async-start(), calls=%async_computation.20 | async-start | bytes 6488064 | tf_op jit(solution)/shard_map/all_gather | solution.py:278
  338.4 26.5 %collective-permute-start.12 = (bf16[128,2048]{1,0:T(8,128)(2,1)}, bf16[128,2048]{1,0:T(8,128)(2,1)}, u32[]{:S(2)}, u32[]{:S(2)}) collective-permute-start(bf16[128,2048]{1,0:T(8,128)(2,1)} %get-tuple-element.218), channel_id=1, source_target_pairs={{0,1},{2,0},{4,2},{6,4},{7,6},{5,7},{3,5},{1,3},{8,9},{10,8},{12,1... | collective-permute-start | bytes 1572872 | tf_op jit(solution)/shard_map/ppermute | solution.py:106
  374.6 46.7 %collective-permute-start.20 = (bf16[1024,2048]{1,0:T(8,128)(2,1)}, bf16[1024,2048]{1,0:T(8,128)(2,1)}, u32[]{:S(2)}, u32[]{:S(2)}) collective-permute-start(bf16[1024,2048]{1,0:T(8,128)(2,1)} %all-gather.15.cloned.1.call-done), channel_id=1, source_target_pairs={{0,8},{8,0},{16,24},{24,16},{1,9},{9,1},{17,25},{25,17},{2,10},{10... | collective-permute-start | bytes 12582920 | tf_op jit(solution)/shard_map/ppermute | solution.py:157
  377.6 117.6 %all-gather.13.cloned.1.call-start = ((), (), s32[]{:S(2)}) async-start(), calls=%async_computation.21 | async-start | bytes 6488064 | tf_op jit(solution)/shard_map/all_gather | solution.py:278
  421.3 198.8 %reduce-scatter.5.cloned.1.call-start = ((), (), s32[]{:S(2)}) async-start(), calls=%async_computation.23 | async-start | bytes 6488064 | tf_op jit(solution)/shard_map/reduce_scatter | solution.py:388
  490.5 212.0 %reduce-scatter.7.cloned.1.call-start = ((), (), s32[]{:S(2)}) async-start(), calls=%async_computation.24 | async-start | bytes 6488064 | tf_op jit(solution)/shard_map/reduce_scatter | solution.py:388
  567.6 180.0 %reduce-scatter.11.cloned.1.call-start = ((), (), s32[]{:S(2)}) async-start(), calls=%async_computation.27 | async-start | bytes 6488064 | tf_op jit(solution)/shard_map/reduce_scatter | solution.py:388
  622.8 42.8 %all-to-all-start.7 = ((bf16[8,352,256]{2,1,0:T(8,128)(2,1)}), bf16[8,352,256]{2,1,0:T(8,128)(2,1)S(1)}, u32[]{:S(2)}, u32[]{:S(2)}) async-start(bf16[8,352,256]{2,1,0:T(8,128)(2,1)} %bitcast.331), calls=%async_computation.8 | async-start | bytes 2883584 | tf_op jit(solution)/shard_map/all_to_all | solution.py:153
  700.7 97.4 %all-gather.17.cloned.1.call-start = ((), (), s32[]{:S(2)}) async-start(), calls=%async_computation.25 | async-start | bytes 4718592 | tf_op jit(solution)/shard_map/all_gather | solution.py:464
  759.1 84.3 %all-to-all-start.9 = ((bf16[8,528,256]{2,1,0:T(8,128)(2,1)}), bf16[8,528,256]{2,1,0:T(8,128)(2,1)}, u32[]{:S(2)}, u32[]{:S(2)}) async-start(bf16[8,528,256]{2,1,0:T(8,128)(2,1)} %pad_maximum_fusion.5), calls=%async_computation.13 | async-start | bytes 4325376 | tf_op jit(solution)/shard_map/all_to_all | solution.py:153
  764.7 280.6 %reduce-scatter.9.cloned.1.call-start = ((), (), s32[]{:S(2)}) async-start(), calls=%async_computation.26 | async-start | bytes 4718592 | tf_op jit(solution)/shard_map/reduce_scatter | solution.py:465
  843.5 38.0 %all-to-all-start.11 = ((bf16[8,64,768]{2,1,0:T(8,128)(2,1)}), bf16[8,64,768]{2,1,0:T(8,128)(2,1)}, u32[]{:S(2)}, u32[]{:S(2)}) async-start(bf16[8,64,768]{2,1,0:T(8,128)(2,1)} %bitcast.94), calls=%async_computation.15 | async-start | bytes 1572864 | tf_op jit(solution)/shard_map/all_to_all | solution.py:153
  881.5 112.7 %all-to-all-start.10 = ((bf16[8,528,256]{2,1,0:T(8,128)(2,1)}), bf16[8,528,256]{2,1,0:T(8,128)(2,1)}, u32[]{:S(2)}, u32[]{:S(2)}) async-start(bf16[8,528,256]{2,1,0:T(8,128)(2,1)} %pad_maximum_fusion.6), calls=%async_computation.14 | async-start | bytes 4325376 | tf_op jit(solution)/shard_map/all_to_all | solution.py:153
  889.0 62.8 %collective-permute-start.34 = (bf16[128,2048]{1,0:T(8,128)(2,1)}, bf16[128,2048]{1,0:T(8,128)(2,1)}, u32[]{:S(2)}, u32[]{:S(2)}) collective-permute-start(bf16[128,2048]{1,0:T(8,128)(2,1)} %pad_maximum_fusion.13), channel_id=1, source_target_pairs={{0,2},{2,4},{4,6},{6,7},{7,5},{5,3},{3,1},{1,0},{8,10},{10,12},{12... | collective-permute-start | bytes 1572872 | tf_op jit(solution)/shard_map/ppermute | solution.py:129
  891.2 60.6 %collective-permute-start.35 = (bf16[128,2048]{1,0:T(8,128)(2,1)S(1)}, bf16[128,2048]{1,0:T(8,128)(2,1)}, u32[]{:S(2)}, u32[]{:S(2)}) collective-permute-start(bf16[128,2048]{1,0:T(8,128)(2,1)S(1)} %pad_maximum_fusion.14), channel_id=1, source_target_pairs={{0,1},{2,0},{4,2},{6,4},{7,6},{5,7},{3,5},{1,3},{8,9},{10,8},{12,1... | collective-permute-start | bytes 1572872 | tf_op jit(solution)/shard_map/ppermute | solution.py:129
  988.3 49.1 %collective-permute-start.37 = (bf16[128,2048]{1,0:T(8,128)(2,1)}, bf16[128,2048]{1,0:T(8,128)(2,1)}, u32[]{:S(2)}, u32[]{:S(2)}) collective-permute-start(bf16[128,2048]{1,0:T(8,128)(2,1)} %get-tuple-element.222), channel_id=1, source_target_pairs={{0,2},{2,4},{4,6},{6,7},{7,5},{5,3},{3,1},{1,0},{8,10},{10,12},{12... | collective-permute-start | bytes 1572872 | tf_op jit(solution)/shard_map/ppermute | solution.py:137
  990.1 47.3 %collective-permute-start.39 = (bf16[128,2048]{1,0:T(8,128)(2,1)}, bf16[128,2048]{1,0:T(8,128)(2,1)}, u32[]{:S(2)}, u32[]{:S(2)}) collective-permute-start(bf16[128,2048]{1,0:T(8,128)(2,1)} %get-tuple-element.221), channel_id=1, source_target_pairs={{0,1},{2,0},{4,2},{6,4},{7,6},{5,7},{3,5},{1,3},{8,9},{10,8},{12,1... | collective-permute-start | bytes 1572872 | tf_op jit(solution)/shard_map/ppermute | solution.py:137
  1000.8 38.4 %all-to-all-start.13 = ((bf16[4,128,1408]{2,1,0:T(8,128)(2,1)}), bf16[4,128,1408]{2,1,0:T(8,128)(2,1)}, u32[]{:S(2)}, u32[]{:S(2)}) async-start(bf16[4,128,1408]{2,1,0:T(8,128)(2,1)} %bitcast.114), calls=%async_computation.17 | async-start | bytes 2883584 | tf_op jit(solution)/shard_map/all_to_all | solution.py:153
  (135 other events, 1656.1 us)
Sparse Core Ops, SparseCore 0:
  11.6 107.2 all-gather.6
  140.9 139.5 all-gather.14
  288.2 59.6 all-gather.8
  377.7 57.1 all-gather.10
  436.9 58.2 all-gather.12
  497.3 55.7 reduce-scatter.4
  567.8 54.9 reduce-scatter.6
  625.1 55.7 reduce-scatter.10
  704.4 90.5 all-gather.16
  799.0 149.4 reduce-scatter.8

commit v2 on v1

--- a/solution.py
+++ b/solution.py
@@ -172,19 +172,6 @@
         whole = lax.dynamic_update_slice_in_dim(whole, came, source * rows, 0)
         whole = lax.dynamic_update_slice_in_dim(whole, sibling(came), (source ^ 1) * rows, 0)
     return whole
-
-
-def reduce_e(blocks):
-    size, at = lax.axis_size(E), lax.axis_index(E)
-    levels, core = size // 2, at % 2
-    blocks = blocks.reshape((levels, 2) + blocks.shape[1:])
-    mine = lax.dynamic_index_in_dim(blocks, core, 1, keepdims=False)
-    theirs = lax.dynamic_index_in_dim(blocks, 1 - core, 1, keepdims=False)
-    mine = mine + sibling(theirs.astype(bf16)).astype(f32)
-    total = pick(mine, at // 2)
-    for by in range(1, levels):
-        total = total + along_y(pick(mine, (at // 2 + by) % levels).astype(bf16), by).astype(f32)
-    return total
 
 
 def after(value, *others):
@@ -248,8 +235,13 @@
     route_rows = vectors[5:]
 
     w_out = lax.all_gather(w_output.astype(bf16), EF, axis=0, tiled=True)
-    qkv_own = jnp.stack([w_query, w_key, w_value]).astype(bf16).reshape(3, part, n_f, slab)
-    qkv_sent = qkv_own.transpose(2, 1, 0, 3).reshape(n_f, part, 3 * slab)
+    qkv_sent = jnp.concatenate(
+        [
+            jnp.concatenate([w[:, f * slab : (f + 1) * slab] for w in (w_query, w_key, w_value)], 1)
+            for f in range(n_f)
+        ]
+    ).astype(bf16)
+    qkv_sent = qkv_sent.reshape(n_f, part, 3 * slab)
     qkv_own = swap_blocks(qkv_sent, F)
     w_qkv = gather_e(qkv_own.reshape(n_f * part, 3 * slab))
 
@@ -258,9 +250,12 @@
         return routed.transpose(1, 0, 2, 3).reshape(n_f, own * per_expert, slab)
 
     def shared_slabs(anchor):
-        two = jnp.stack([after(shared_wgate, anchor), shared_wup]).astype(bf16)
-        two = two.reshape(2, part, n_e, n_f * per_shared).transpose(2, 0, 1, 3)
-        return two.reshape(n_e, 2 * part, n_f * per_shared)
+        columns = n_f * per_shared
+        gate = after(shared_wgate, anchor)
+        two = jnp.concatenate(
+            [w[:, e * columns : (e + 1) * columns] for e in range(n_e) for w in (gate, shared_wup)]
+        )
+        return two.astype(bf16).reshape(n_e, 2 * part, columns)
 
     routed_down = expert_wdown.astype(bf16).reshape(own, n_f, per_expert, slab)
     routed_down = routed_down.transpose(1, 0, 2, 3).reshape(n_f, own * per_expert, slab)
@@ -461,10 +456,8 @@
     gate_back = swap_blocks(after(gate_slabs(d_gate), mixed_grad), F)
     up_back = swap_blocks(after(gate_slabs(d_up), gate_back), F)
     mixed_grad = mixed_grad.reshape(seq, slab)
-    hidden_low = lax.all_gather(after(hidden_low, d_up), F, axis=0, tiled=True)
-    moe = lax.psum_scatter(after(moe, hidden_low), F, scatter_dimension=0, tiled=True)
+    moe = lax.psum_scatter(after(moe, d_up, ffn_grad), F, scatter_dimension=0, tiled=True)
     output = (hidden + moe.astype(f32)).astype(bf16)
-    d_out = contract(mixed, hidden_low)
     lin_grads = [[], [], []]
     for h in range(heads):
         q, k, v, probs = saved[h]
@@ -481,7 +474,9 @@
     normed_part = product_t(lin_grad, w_qkv).astype(bf16)
     d_qkv = contract(normed, lin_grad)
     d_expert_gate, d_expert_up = return_gate(gate_back), return_gate(up_back)
-    normed_grad = ring_scatter(normed_part, {3: d_qkv, 2: d_expert_gate, 0: up_back})
+    normed_grad = ring_scatter(normed_part, {3: d_qkv, 1: gate_back})
+    hidden_low = lax.all_gather(after(hidden_low, moe, normed_part), F, axis=0, tiled=True)
+    d_out = contract(mixed, hidden_low)
     d_bias = jnp.sum(lin_grad.astype(f32), axis=0).reshape(3, slab)
     d_gain_one = jnp.sum(d_qkv * w_qkv.astype(f32), axis=1) / gain_one
     token_back, unused = norm_back(tokens.astype(f32), gain_one, normed_grad)
@@ -496,9 +491,9 @@
     shared_two = shared_two.reshape(2, part, devices * per_shared).astype(f32)
 
     from_heads = [(e * n_f + f, n_e * f + e) for e in range(n_e) for f in range(n_f)]
-    d_out = reduce_e(d_out.reshape(n_e, part, width)).astype(bf16)
+    d_out = lax.psum_scatter(d_out.astype(bf16), E, scatter_dimension=0, tiled=True)
     d_wout = lax.ppermute(d_out, EF, from_heads).astype(f32)
-    d_qkv = reduce_e(d_qkv.reshape(n_e, n_f * part, 3 * slab)).astype(bf16)
+    d_qkv = lax.psum_scatter(d_qkv.astype(bf16), E, scatter_dimension=0, tiled=True)
     d_qkv = swap_blocks(d_qkv.reshape(n_f, part, 3 * slab), F)
     d_qkv = d_qkv.reshape(n_f, part, 3, slab).transpose(2, 1, 0, 3).reshape(3, part, width)
     d_qkv = d_qkv.astype(f32)

time: 1070 us -> 1080 us (level)
  blocking collectives: 0 us -> 31.7 us
  waiting for transfers between devices: 374 us -> 393 us
  local copies, waits for them, and re-layouts: 172 us -> 156 us
  starting transfers between devices: 177 us -> 162 us
    ppermute x16, waiting for transfers between devices: 103 us -> 143 us  [ring_scatter(): up, down = (lax.ppermute(up, F, right), lax.ppermute(down, F, left))]
    all_to_all x14 -> x13, waiting for transfers between devices: 183 us -> 145 us  [swap_blocks(): return lax.all_to_all(blocks, axis, split_axis=0, concat_axis=0, tiled=True)]
    reduce_scatter x1 -> x3, waiting for transfers between devices: 0.01 us -> 34.5 us  [the longest x1 34.5 us: shards(): lax.psum_scatter(after(moe, d_up, ffn_grad), F, scatter_dimension=0, tile...]
    all_to_all x0 -> x1, blocking collectives: none -> 31.7 us  [swap_blocks(): return lax.all_to_all(blocks, axis, split_axis=0, concat_axis=0, tiled=True)]
    ppermute x3 -> x1, waiting for transfers between devices: 29.2 us -> 10.9 us  [along_y(): lax.ppermute(value, E, [(e, (e + 2 * by) % size) for e in range(size)])]
    all_to_all x14 -> x13, starting transfers between devices: 92 us -> 74 us  [swap_blocks(): return lax.all_to_all(blocks, axis, split_axis=0, concat_axis=0, tiled=True)]
    all_gather x3, starting transfers between devices: 0.12 us -> 12.6 us  [both_levels(): lax.all_gather(mine, E, axis=0, tiled=True, axis_index_groups=along_levels)]
    unnamed x210 -> x206, local copies, waits for them, and re-layouts: 41.8 us -> 36.3 us
  transfers between devices with their start and end apart: 69 -> 66, of which waited for: 27 -> 26; matrix products, arithmetic and copies ran while one was open for 43% -> 41% of each run, Pallas kernels for 0% -> 0%
where the time goes in v2:
time: 1080 us; the launch traced here: 1070 us
  waiting for transfers between devices  393 us (36%)
  matrix products  235 us (22%)
  starting transfers between devices  162 us (15%)
  local copies, waits for them, and re-layouts  156 us (14%)
  other arithmetic  65.7 us (6%)
  blocking collectives  31.7 us (3%)
  between operations  28.8 us (3%)
    dot_general x35, matrix products, dot(): lax.dot_general(left, right, (((left_dim,), (right_dim,)), ((), ())), pre...  235 us
    all_to_all x13, waiting for transfers between devices, swap_blocks(): return lax.all_to_all(blocks, axis, split_axis=0, concat_axis=0, tiled=True)  145 us
    ppermute x16, waiting for transfers between devices, ring_scatter(): up, down = (lax.ppermute(up, F, right), lax.ppermute(down, F, left))  143 us
    all_to_all x13, starting transfers between devices, swap_blocks(): return lax.all_to_all(blocks, axis, split_axis=0, concat_axis=0, tiled=True)  74 us
    unnamed x206, local copies, waits for them, and re-layouts  36.3 us
    ppermute x12, waiting for transfers between devices, ring_gather(): up, down = (lax.ppermute(up, F, right), lax.ppermute(down, F, left))  35.7 us
    reduce_scatter x1, waiting for transfers between devices, shards(): lax.psum_scatter(after(moe, d_up, ffn_grad), F, scatter_dimension=0, tile...  34.5 us
    ppermute x16, starting transfers between devices, ring_scatter(): up, down = (lax.ppermute(up, F, right), lax.ppermute(down, F, left))  33.3 us
  transfers between devices with their start and end apart: 66, of which 26 were waited for; matrix products, arithmetic and copies ran while one was open for 41% of the time, Pallas kernels for 0%

profile of v2, /device:TPU:1, one launch (start us, length us, event | category | flops | bytes accessed | tf_op | source)
XLA Modules:
  0.0 1071.1 jit_solution(7912241356067412562)
XLA Ops:
  93.4 11.2 %all-to-all-start.2 = ((bf16[32,2,704]{2,1,0:T(2,128)(2,1)}), bf16[32,2,704]{2,1,0:T(2,128)(2,1)}, u32[]{:S(2)}, u32[]{:S(2)}) async-start(bf16[32,2,704]{2,1,0:T(2,128)(2,1)} %reshape.556), calls=%async_computation.2 | async-start | bytes 196608 | tf_op jit(solution)/shard_map/all_to_all | solution.py:153
  104.6 10.4 collective-permute-done.5
  146.3 10.9 %collective-permute-done.9 = bf16[512,768]{0,1:T(8,128)(2,1)S(1)} collective-permute-done((bf16[512,768]{0,1:T(8,128)(2,1)S(1)}, bf16[512,768]{0,1:T(8,128)(2,1)S(1)}, u32[]{:S(2)}, u32[]{:S(2)}) %collective-permute-start.9) | collective-permute-done | bytes 786464 | tf_op jit(solution)/shard_map/ppermute | solution.py:162
  180.1 100.5 %all-to-all-done.3 = bf16[8,1056,256]{2,1,0:T(8,128)(2,1)} async-done(((bf16[8,1056,256]{2,1,0:T(8,128)(2,1)}), bf16[8,1056,256]{2,1,0:T(8,128)(2,1)}, u32[]{:S(2)}, u32[]{:S(2)}) %all-to-all-start.3) | async-done | bytes 4325408 | tf_op jit(solution)/shard_map/all_to_all | solution.py:153
  299.0 13.4 %all-to-all-done.4 = bf16[8,128,256]{1,2,0:T(8,128)(2,1)S(1)} async-done(((bf16[8,128,256]{1,2,0:T(8,128)(2,1)}), bf16[8,128,256]{1,2,0:T(8,128)(2,1)S(1)}, u32[]{:S(2)}, u32[]{:S(2)}) %all-to-all-start.4) | async-done | bytes 524320 | tf_op jit(solution)/shard_map/all_to_all | solution.py:153
  317.2 12.3 %all-gather.11.cloned.1.call-start = ((), (), s32[]{:S(2)}) async-start(), calls=%async_computation.22 | async-start | bytes 6488064 | tf_op jit(solution)/shard_map/all_gather | solution.py:273
  345.6 7.4 collective-permute-done.11
  420.1 15.5 %fusion.126 = f32[2048,1056]{0,1:T(8,128)} fusion(bf16[1056,2048]{1,0:T(8,128)(2,1)} %all-gather.9.cloned.1.call-done, bf16[1024,2048]{1,0:T(8,128)(2,1)} %collective-permute-done.19, bf16[1024,2048]{1,0:T(8,128)(2,1)} %constant_dynamic-update-slice_fusion.15), kind=kOutput, calls=%fused_computation.327 | convolution fusion | flops 8875147264 | bytes 21364736 | tf_op jit(solution)/shard_map/dot_general | solution.py:22
  435.6 15.9 %fusion.125 = f32[2048,1056]{0,1:T(8,128)} fusion(bf16[1056,2048]{1,0:T(8,128)(2,1)} %all-gather.11.cloned.1.call-done, bf16[1024,2048]{1,0:T(8,128)(2,1)} %collective-permute-done.19, bf16[1024,2048]{1,0:T(8,128)(2,1)} %constant_dynamic-update-slice_fusion.15), kind=kOutput, calls=%fused_computation.326 | convolution fusion | flops 8875147264 | bytes 21364736 | tf_op jit(solution)/shard_map/dot_general | solution.py:22
  451.7 12.0 %fusion = (bf16[2048,1056]{0,1:T(8,128)(2,1)S(1)}, bf16[2048,1056]{0,1:T(8,128)(2,1)}, f32[2048,1056]{0,1:T(8,128)}) fusion(f32[2048,1056]{0,1:T(8,128)} %fusion.125, f32[2048,1056]{0,1:T(8,128)} %fusion.126, f32[2048,12]{0,1:T(8,128)S(1)} %reshape.516, s32[1056]{0:T(1024)S(1)} %fusion.94), kind=kOutput, calls=%fused_computation.4 | convolution fusion | flops 330903936 | bytes 34705536 | tf_op jit(solution)/shard_map/dot_general | solution.py:22
  465.7 13.3 %convolution_convert_fusion.2 = bf16[1056,2048]{1,0:T(8,128)(2,1)} fusion(bf16[2048,1056]{0,1:T(8,128)(2,1)S(1)} %get-tuple-element.90, bf16[2048,2048]{1,0:T(8,128)(2,1)} %constant_dynamic-update-slice_fusion), kind=kOutput, calls=%fused_computation.20 | convolution fusion | flops 8860532736 | bytes 17039360 | tf_op jit(solution)/shard_map/dot_general | solution.py:22
  482.2 24.5 %multiply_convert_fusion = (bf16[2048,1056]{0,1:T(8,128)(2,1)}, bf16[2048,1056]{0,1:T(8,128)(2,1)}, f32[2048,1056]{0,1:T(8,128)}) fusion(f32[2048,1056]{0,1:T(8,128)} %get-tuple-element.346, f32[2048,1056]{0,1:T(8,128)} %fusion.126, f32[2048,1056]{0,1:T(8,128)} %fusion.125, bf16[2048,2048]{1,0:T(8,128)(2,1)} %constant_dynamic-update-slice_fusion, ...), kind=kOutput, calls=%fused_computation.6 | convolution fusion | flops 8888647680 | bytes 55967744 | tf_op jit(solution)/shard_map/dot_general | solution.py:22
  506.7 14.3 %convolution_convert_fusion = bf16[1056,2048]{1,0:T(8,128)(2,1)} fusion(bf16[2048,1056]{0,1:T(8,128)(2,1)} %get-tuple-element.89, bf16[1024,2048]{1,0:T(8,128)(2,1)} %collective-permute-done.19, bf16[1024,2048]{1,0:T(8,128)(2,1)} %constant_dynamic-update-slice_fusion.15), kind=kOutput, calls=%fused_computation.18 | convolution fusion | flops 8877309952 | bytes 17039360 | tf_op jit(solution)/shard_map/dot_general | solution.py:22
  521.1 14.5 %convolution_convert_fusion.1 = bf16[1056,2048]{1,0:T(8,128)(2,1)} fusion(bf16[2048,1056]{0,1:T(8,128)(2,1)} %get-tuple-element.88, bf16[1024,2048]{1,0:T(8,128)(2,1)} %collective-permute-done.19, bf16[1024,2048]{1,0:T(8,128)(2,1)} %constant_dynamic-update-slice_fusion.15), kind=kOutput, calls=%fused_computation.19 | convolution fusion | flops 8877309952 | bytes 17039360 | tf_op jit(solution)/shard_map/dot_general | solution.py:22
  535.5 8.2 fusion.18
  543.8 9.8 add_convert_fusion.2
  554.7 8.3 fusion.21
  563.0 10.6 add_convert_fusion.1
  573.6 7.2 convolution_convert_fusion.4
  581.1 8.2 fusion.1
  613.4 10.8 %add_convert_fusion = bf16[1024,2048]{1,0:T(8,128)(2,1)} fusion(bf16[1024,2048]{1,0:T(8,128)(2,1)} %collective-permute-done.22, bf16[1056,2048]{1,0:T(8,128)(2,1)} %all-gather.13.cloned.1.call-done, bf16[2048,1056]{0,1:T(8,128)(2,1)} %copy-done.84), kind=kOutput, calls=%fused_computation.15 | convolution fusion | flops 4435476480 | bytes 14876672 | tf_op jit(solution)/shard_map/dot_general | solution.py:22
  627.4 21.6 %collective-permute-done.28 = bf16[128,2048]{1,0:T(8,128)(2,1)S(1)} collective-permute-done((bf16[128,2048]{1,0:T(8,128)(2,1)S(1)}, bf16[128,2048]{1,0:T(8,128)(2,1)S(1)}, u32[]{:S(2)}, u32[]{:S(2)}) %collective-permute-start.28) | collective-permute-done | bytes 524320 | tf_op jit(solution)/shard_map/ppermute | solution.py:129
  655.7 8.7 collective-permute-start.30
  684.2 31.7 %all_to_all.70 = bf16[8,128,256]{2,1,0:T(8,128)(2,1)S(1)} all-to-all(bf16[8,128,256]{2,1,0:T(8,128)(2,1)S(1)} %bitcast.330), channel_id=1, replica_groups=mesh['expert'=4,'fsdp'=8] {'fsdp'}, dimensions={0} | all-to-all | bytes 1048576 | tf_op jit(solution)/shard_map/all_to_all | solution.py:153
  728.6 8.7 multiply_reduce_fusion
  753.5 7.8 convolution_convert_fusion.3
  761.4 34.5 %reduce-scatter.11.cloned.1.call-done = bf16[128,2048]{1,0:T(8,128)(2,1)} async-done(((bf16[1024,2048]{1,0:T(8,128)(2,1)}), bf16[128,2048]{1,0:T(8,128)(2,1)}) %reduce-scatter.11.cloned.1.call-update) | async-done | bytes 524304 | tf_op jit(solution)/shard_map/reduce_scatter | solution.py:459
  801.3 15.3 %all-to-all-done.9 = bf16[8,528,256]{2,1,0:T(8,128)(2,1)} async-done(((bf16[8,528,256]{2,1,0:T(8,128)(2,1)}), bf16[8,528,256]{2,1,0:T(8,128)(2,1)}, u32[]{:S(2)}, u32[]{:S(2)}) %all-to-all-start.9) | async-done | bytes 2162720 | tf_op jit(solution)/shard_map/all_to_all | solution.py:153
  844.6 48.9 %collective-permute-done.36 = bf16[128,2048]{1,0:T(8,128)(2,1)S(1)} collective-permute-done((bf16[128,2048]{1,0:T(8,128)(2,1)S(1)}, bf16[128,2048]{1,0:T(8,128)(2,1)S(1)}, u32[]{:S(2)}, u32[]{:S(2)}) %collective-permute-start.36) | collective-permute-done | bytes 524320 | tf_op jit(solution)/shard_map/ppermute | solution.py:129
  894.7 11.5 %collective-permute-start.37 = (bf16[128,2048]{1,0:T(8,128)(2,1)S(1)}, bf16[128,2048]{1,0:T(8,128)(2,1)S(1)}, u32[]{:S(2)}, u32[]{:S(2)}) collective-permute-start(bf16[128,2048]{1,0:T(8,128)(2,1)S(1)} %add_convert_fusion.4), channel_id=1, source_target_pairs={{0,1},{2,0},{4,2},{6,4},{7,6},{5,7},{3,5},{1,3},{8,9},{10,8},{12,1... | collective-permute-start | bytes 1572872 | tf_op jit(solution)/shard_map/ppermute | solution.py:129
  906.2 52.6 %collective-permute-done.37 = bf16[128,2048]{1,0:T(8,128)(2,1)S(1)} collective-permute-done((bf16[128,2048]{1,0:T(8,128)(2,1)S(1)}, bf16[128,2048]{1,0:T(8,128)(2,1)S(1)}, u32[]{:S(2)}, u32[]{:S(2)}) %collective-permute-start.37) | collective-permute-done | bytes 524320 | tf_op jit(solution)/shard_map/ppermute | solution.py:129
  1047.6 15.5 %collective-permute-done.40 = bf16[64,2048]{1,0:T(8,128)(2,1)S(1)} collective-permute-done((bf16[64,2048]{1,0:T(8,128)(2,1)}, bf16[64,2048]{1,0:T(8,128)(2,1)S(1)}, u32[]{:S(2)}, u32[]{:S(2)}) %collective-permute-start.40) | collective-permute-done | bytes 262176 | tf_op jit(solution)/shard_map/ppermute | solution.py:495
  (589 shorter events, 446.3 us)
Async XLA Ops:
  7.2 322.3 %all-gather.7.cloned.1.call-start = ((), (), s32[]{:S(2)}) async-start(), calls=%async_computation.20 | async-start | bytes 8650752 | tf_op jit(solution)/shard_map/all_gather | solution.py:237
  9.1 29.2 %collective-permute-start = (bf16[128,2048]{1,0:T(8,128)(2,1)}, bf16[128,2048]{1,0:T(8,128)(2,1)}, u32[]{:S(2)}, u32[]{:S(2)}) collective-permute-start(bf16[128,2048]{1,0:T(8,128)(2,1)} %param.88), channel_id=1, source_target_pairs={{0,2},{2,4},{4,6},{6,7},{7,5},{5,3},{3,1},{1,0},{8,10},{10,12},{12... | collective-permute-start | bytes 1572872 | tf_op jit(solution)/shard_map/ppermute | solution.py:106
  11.3 27.1 %collective-permute-start.1 = (bf16[128,2048]{1,0:T(8,128)(2,1)}, bf16[128,2048]{1,0:T(8,128)(2,1)}, u32[]{:S(2)}, u32[]{:S(2)}) collective-permute-start(bf16[128,2048]{1,0:T(8,128)(2,1)} %param.88), channel_id=1, source_target_pairs={{0,1},{2,0},{4,2},{6,4},{7,6},{5,7},{3,5},{1,3},{8,9},{10,8},{12,1... | collective-permute-start | bytes 1572872 | tf_op jit(solution)/shard_map/ppermute | solution.py:106
  14.2 45.7 %all-to-all-start.1 = ((bf16[4,128,1408]{2,1,0:T(8,128)(2,1)}), bf16[4,128,1408]{2,1,0:T(8,128)(2,1)S(1)}, u32[]{:S(2)}, u32[]{:S(2)}) async-start(bf16[4,128,1408]{2,1,0:T(8,128)(2,1)} %bitcast.334), calls=%async_computation.1 | async-start | bytes 2883584 | tf_op jit(solution)/shard_map/all_to_all | solution.py:153
  38.4 31.1 %collective-permute-start.2 = (bf16[128,2048]{1,0:T(8,128)(2,1)}, bf16[128,2048]{1,0:T(8,128)(2,1)}, u32[]{:S(2)}, u32[]{:S(2)}) collective-permute-start(bf16[128,2048]{1,0:T(8,128)(2,1)} %collective-permute-done), channel_id=1, source_target_pairs={{0,2},{2,4},{4,6},{6,7},{7,5},{5,3},{3,1},{1,0},{8,10},{10,12},{12... | collective-permute-start | bytes 1572872 | tf_op jit(solution)/shard_map/ppermute | solution.py:106
  40.1 29.4 %collective-permute-start.3 = (bf16[128,2048]{1,0:T(8,128)(2,1)}, bf16[128,2048]{1,0:T(8,128)(2,1)}, u32[]{:S(2)}, u32[]{:S(2)}) collective-permute-start(bf16[128,2048]{1,0:T(8,128)(2,1)} %collective-permute-done.1), channel_id=1, source_target_pairs={{0,1},{2,0},{4,2},{6,4},{7,6},{5,7},{3,5},{1,3},{8,9},{10,8},{12,1... | collective-permute-start | bytes 1572872 | tf_op jit(solution)/shard_map/ppermute | solution.py:106
  60.0 33.5 %all-to-all-start = ((bf16[8,64,768]{2,1,0:T(8,128)(2,1)}), bf16[8,64,768]{2,1,0:T(8,128)(2,1)S(1)}, u32[]{:S(2)}, u32[]{:S(2)}) async-start(bf16[8,64,768]{2,1,0:T(8,128)(2,1)} %bitcast.3), calls=%async_computation | async-start | bytes 1572864 | tf_op jit(solution)/shard_map/all_to_all | solution.py:153
  69.5 35.1 %collective-permute-start.4 = (bf16[128,2048]{1,0:T(8,128)(2,1)}, bf16[128,2048]{1,0:T(8,128)(2,1)}, u32[]{:S(2)}, u32[]{:S(2)}) collective-permute-start(bf16[128,2048]{1,0:T(8,128)(2,1)} %collective-permute-done.2), channel_id=1, source_target_pairs={{0,2},{2,4},{4,6},{6,7},{7,5},{5,3},{3,1},{1,0},{8,10},{10,12},{12... | collective-permute-start | bytes 1572872 | tf_op jit(solution)/shard_map/ppermute | solution.py:106
  71.0 44.0 %collective-permute-start.5 = (bf16[128,2048]{1,0:T(8,128)(2,1)}, bf16[128,2048]{1,0:T(8,128)(2,1)}, u32[]{:S(2)}, u32[]{:S(2)}) collective-permute-start(bf16[128,2048]{1,0:T(8,128)(2,1)} %collective-permute-done.3), channel_id=1, source_target_pairs={{0,1},{2,0},{4,2},{6,4},{7,6},{5,7},{3,5},{1,3},{8,9},{10,8},{12,1... | collective-permute-start | bytes 1572872 | tf_op jit(solution)/shard_map/ppermute | solution.py:106
  93.4 37.7 %all-to-all-start.2 = ((bf16[32,2,704]{2,1,0:T(2,128)(2,1)}), bf16[32,2,704]{2,1,0:T(2,128)(2,1)}, u32[]{:S(2)}, u32[]{:S(2)}) async-start(bf16[32,2,704]{2,1,0:T(2,128)(2,1)} %reshape.556), calls=%async_computation.2 | async-start | bytes 196608 | tf_op jit(solution)/shard_map/all_to_all | solution.py:153
  131.1 149.5 %all-to-all-start.3 = ((bf16[8,1056,256]{2,1,0:T(8,128)(2,1)}), bf16[8,1056,256]{2,1,0:T(8,128)(2,1)}, u32[]{:S(2)}, u32[]{:S(2)}) async-start(bf16[8,1056,256]{2,1,0:T(8,128)(2,1)} %pad_maximum_fusion.1), calls=%async_computation.3 | async-start | bytes 8650752 | tf_op jit(solution)/shard_map/all_to_all | solution.py:153
  136.0 226.5 %all-gather.15.cloned.1.call-start = ((), (), s32[]{:S(2)}) async-start(), calls=%async_computation.24 | async-start | bytes 4718592 | tf_op jit(solution)/shard_map/all_gather | solution.py:303
  136.7 283.4 %all-gather.9.cloned.1.call-start = ((), (), s32[]{:S(2)}) async-start(), calls=%async_computation.21 | async-start | bytes 6488064 | tf_op jit(solution)/shard_map/all_gather | solution.py:273
  312.4 67.9 %all-to-all-start.5 = ((bf16[8,352,256]{2,1,0:T(8,128)(2,1)}), bf16[8,352,256]{2,1,0:T(8,128)(2,1)S(1)}, u32[]{:S(2)}, u32[]{:S(2)}) async-start(bf16[8,352,256]{2,1,0:T(8,128)(2,1)} %bitcast.28), calls=%async_computation.5 | async-start | bytes 2883584 | tf_op jit(solution)/shard_map/all_to_all | solution.py:153
  317.2 118.4 %all-gather.11.cloned.1.call-start = ((), (), s32[]{:S(2)}) async-start(), calls=%async_computation.22 | async-start | bytes 6488064 | tf_op jit(solution)/shard_map/all_gather | solution.py:273
  362.4 47.9 %collective-permute-start.20 = (bf16[1024,2048]{1,0:T(8,128)(2,1)}, bf16[1024,2048]{1,0:T(8,128)(2,1)}, u32[]{:S(2)}, u32[]{:S(2)}) collective-permute-start(bf16[1024,2048]{1,0:T(8,128)(2,1)} %all-gather.15.cloned.1.call-done), channel_id=1, source_target_pairs={{0,8},{8,0},{16,24},{24,16},{1,9},{9,1},{17,25},{25,17},{2,10},{10... | collective-permute-start | bytes 12582920 | tf_op jit(solution)/shard_map/ppermute | solution.py:157
  364.4 117.9 %all-gather.13.cloned.1.call-start = ((), (), s32[]{:S(2)}) async-start(), calls=%async_computation.23 | async-start | bytes 6488064 | tf_op jit(solution)/shard_map/all_gather | solution.py:273
  410.2 196.5 %reduce-scatter.9.cloned.1.call-start = ((), (), s32[]{:S(2)}) async-start(), calls=%async_computation.26 | async-start | bytes 6488064 | tf_op jit(solution)/shard_map/reduce_scatter | solution.py:383
  479.0 198.1 %reduce-scatter.7.cloned.1.call-start = ((), (), s32[]{:S(2)}) async-start(), calls=%async_computation.25 | async-start | bytes 6488064 | tf_op jit(solution)/shard_map/reduce_scatter | solution.py:383
  521.0 216.3 %reduce-scatter.13.cloned.1.call-start = ((), (), s32[]{:S(2)}) async-start(), calls=%async_computation.28 | async-start | bytes 6488064 | tf_op jit(solution)/shard_map/reduce_scatter | solution.py:383
  580.9 24.4 %collective-permute-start.22 = (bf16[1024,2048]{1,0:T(8,128)(2,1)}, bf16[1024,2048]{1,0:T(8,128)(2,1)}, u32[]{:S(2)}, u32[]{:S(2)}) collective-permute-start(bf16[1024,2048]{1,0:T(8,128)(2,1)} %convolution_convert_fusion.4), channel_id=1, source_target_pairs={{0,8},{8,0},{16,24},{24,16},{1,9},{9,1},{17,25},{25,17},{2,10},{10... | collective-permute-start | bytes 12582920 | tf_op jit(solution)/shard_map/ppermute | solution.py:157
  609.7 43.8 %all-to-all-start.7 = ((bf16[8,352,256]{2,1,0:T(8,128)(2,1)}), bf16[8,352,256]{2,1,0:T(8,128)(2,1)S(1)}, u32[]{:S(2)}, u32[]{:S(2)}) async-start(bf16[8,352,256]{2,1,0:T(8,128)(2,1)} %bitcast.292), calls=%async_computation.9 | async-start | bytes 2883584 | tf_op jit(solution)/shard_map/all_to_all | solution.py:153
  613.3 182.6 %reduce-scatter.11.cloned.1.call-start = ((), (), s32[]{:S(2)}) async-start(), calls=%async_computation.27 | async-start | bytes 4718592 | tf_op jit(solution)/shard_map/reduce_scatter | solution.py:459
  677.2 293.5 %reduce-scatter.15.cloned.1.call-start = ((), (), s32[]{:S(2)}) async-start(), calls=%async_computation.29 | async-start | bytes 3932160 | tf_op jit(solution)/shard_map/reduce_scatter | solution.py:496
  748.8 67.8 %all-to-all-start.9 = ((bf16[8,528,256]{2,1,0:T(8,128)(2,1)}), bf16[8,528,256]{2,1,0:T(8,128)(2,1)}, u32[]{:S(2)}, u32[]{:S(2)}) async-start(bf16[8,528,256]{2,1,0:T(8,128)(2,1)} %pad_maximum_fusion.5), calls=%async_computation.13 | async-start | bytes 4325376 | tf_op jit(solution)/shard_map/all_to_all | solution.py:153
  753.3 237.0 %all-gather.17.cloned.1.call-start = ((), (), s32[]{:S(2)}) async-start(), calls=%async_computation.30 | async-start | bytes 4718592 | tf_op jit(solution)/shard_map/all_gather | solution.py:478
  835.8 137.3 %all-to-all-start.12 = ((bf16[8,528,256]{2,1,0:T(8,128)(2,1)}), bf16[8,528,256]{2,1,0:T(8,128)(2,1)}, u32[]{:S(2)}, u32[]{:S(2)}) async-start(bf16[8,528,256]{2,1,0:T(8,128)(2,1)} %pad_maximum_fusion.6), calls=%async_computation.18 | async-start | bytes 4325376 | tf_op jit(solution)/shard_map/all_to_all | solution.py:153
  843.0 50.5 %collective-permute-start.36 = (bf16[128,2048]{1,0:T(8,128)(2,1)S(1)}, bf16[128,2048]{1,0:T(8,128)(2,1)S(1)}, u32[]{:S(2)}, u32[]{:S(2)}) collective-permute-start(bf16[128,2048]{1,0:T(8,128)(2,1)S(1)} %pad_maximum_fusion.13), channel_id=1, source_target_pairs={{0,1},{2,0},{4,2},{6,4},{7,6},{5,7},{3,5},{1,3},{8,9},{10,8},{12,1... | collective-permute-start | bytes 1572872 | tf_op jit(solution)/shard_map/ppermute | solution.py:129
  844.5 61.6 %collective-permute-start.34 = (bf16[128,2048]{1,0:T(8,128)(2,1)S(1)}, bf16[128,2048]{1,0:T(8,128)(2,1)S(1)}, u32[]{:S(2)}, u32[]{:S(2)}) collective-permute-start(bf16[128,2048]{1,0:T(8,128)(2,1)S(1)} %pad_maximum_fusion.12), channel_id=1, source_target_pairs={{0,2},{2,4},{4,6},{6,7},{7,5},{5,3},{3,1},{1,0},{8,10},{10,12},{12... | collective-permute-start | bytes 1572872 | tf_op jit(solution)/shard_map/ppermute | solution.py:129
  894.7 64.1 %collective-permute-start.37 = (bf16[128,2048]{1,0:T(8,128)(2,1)S(1)}, bf16[128,2048]{1,0:T(8,128)(2,1)S(1)}, u32[]{:S(2)}, u32[]{:S(2)}) collective-permute-start(bf16[128,2048]{1,0:T(8,128)(2,1)S(1)} %add_convert_fusion.4), channel_id=1, source_target_pairs={{0,1},{2,0},{4,2},{6,4},{7,6},{5,7},{3,5},{1,3},{8,9},{10,8},{12,1... | collective-permute-start | bytes 1572872 | tf_op jit(solution)/shard_map/ppermute | solution.py:129
  973.1 40.6 %all-to-all-start.10 = ((bf16[8,64,768]{2,1,0:T(8,128)(2,1)}), bf16[8,64,768]{2,1,0:T(8,128)(2,1)}, u32[]{:S(2)}, u32[]{:S(2)}) async-start(bf16[8,64,768]{2,1,0:T(8,128)(2,1)} %bitcast.79), calls=%async_computation.15 | async-start | bytes 1572864 | tf_op jit(solution)/shard_map/all_to_all | solution.py:153
  978.4 60.9 %reduce-scatter.17.cloned.1.call-start = ((), (), s32[]{:S(2)}) async-start(), calls=%async_computation.31 | async-start | bytes 1310720 | tf_op jit(solution)/shard_map/reduce_scatter | solution.py:494
  (128 other events, 2146.1 us)
Sparse Core Ops, SparseCore 0:
  11.6 105.6 all-gather.6
  138.9 139.5 all-gather.14
  286.3 59.6 all-gather.8
  364.5 57.4 all-gather.10
  424.0 58.2 all-gather.12
  484.4 55.7 reduce-scatter.8
  542.6 55.7 reduce-scatter.6
  600.6 55.7 reduce-scatter.12
  677.3 118.5 reduce-scatter.10
  798.3 48.6 reduce-scatter.14
  850.0 107.9 all-gather.16
  995.1 27.8 reduce-scatter.16

commit v3 on v2

--- a/solution.py
+++ b/solution.py
@@ -453,10 +453,9 @@
     hidden_low = hidden_grad.astype(bf16)
     mixed_grad = product_t(hidden_low, w_out).astype(bf16).reshape(rows, n_f, slab)
     mixed_grad = swap_blocks(mixed_grad.transpose(1, 0, 2), F)
-    gate_back = swap_blocks(after(gate_slabs(d_gate), mixed_grad), F)
-    up_back = swap_blocks(after(gate_slabs(d_up), gate_back), F)
     mixed_grad = mixed_grad.reshape(seq, slab)
-    moe = lax.psum_scatter(after(moe, d_up, ffn_grad), F, scatter_dimension=0, tiled=True)
+    hidden_low = lax.all_gather(after(hidden_low, d_up), F, axis=0, tiled=True)
+    moe = lax.psum_scatter(after(moe, hidden_low), F, scatter_dimension=0, tiled=True)
     output = (hidden + moe.astype(f32)).astype(bf16)
     lin_grads = [[], [], []]
     for h in range(heads):
@@ -472,10 +471,11 @@
         lin_grads[2].append(contract(probs.astype(bf16), out_grad).astype(bf16))
     lin_grad = jnp.concatenate(lin_grads[0] + lin_grads[1] + lin_grads[2], axis=1)
     normed_part = product_t(lin_grad, w_qkv).astype(bf16)
+    gate_back = swap_blocks(after(gate_slabs(d_gate), normed_part), F)
+    up_back = swap_blocks(after(gate_slabs(d_up), gate_back), F)
     d_qkv = contract(normed, lin_grad)
     d_expert_gate, d_expert_up = return_gate(gate_back), return_gate(up_back)
-    normed_grad = ring_scatter(normed_part, {3: d_qkv, 1: gate_back})
-    hidden_low = lax.all_gather(after(hidden_low, moe, normed_part), F, axis=0, tiled=True)
+    normed_grad = ring_scatter(normed_part, {3: d_qkv})
     d_out = contract(mixed, hidden_low)
     d_bias = jnp.sum(lin_grad.astype(f32), axis=0).reshape(3, slab)
     d_gain_one = jnp.sum(d_qkv * w_qkv.astype(f32), axis=1) / gain_one

time: 1080 us -> 1060 us (0.981)
  blocking collectives: 31.7 us -> 0 us
  starting transfers between devices: 162 us -> 187 us
  waiting for transfers between devices: 393 us -> 371 us
    all_gather x1, waiting for transfers between devices: 0.02 us -> 56.6 us  [shards(): hidden_low = lax.all_gather(after(hidden_low, d_up), F, axis=0, tiled=True)]
    reduce_scatter x1, waiting for transfers between devices: 34.5 us -> 0.01 us  [shards(): lax.psum_scatter(after(moe, hidden_low), F, scatter_dimension=0, tiled=True)]
    all_to_all x1 -> x0, blocking collectives: 31.7 us -> none  [swap_blocks(): return lax.all_to_all(blocks, axis, split_axis=0, concat_axis=0, tiled=True)]
    ppermute x16, waiting for transfers between devices: 143 us -> 115 us  [ring_scatter(): up, down = (lax.ppermute(up, F, right), lax.ppermute(down, F, left))]
    ppermute x16, starting transfers between devices: 33.3 us -> 52.8 us  [ring_scatter(): up, down = (lax.ppermute(up, F, right), lax.ppermute(down, F, left))]
    all_to_all x13 -> x14, waiting for transfers between devices: 145 us -> 136 us  [swap_blocks(): return lax.all_to_all(blocks, axis, split_axis=0, concat_axis=0, tiled=True)]
    all_to_all x13 -> x14, starting transfers between devices: 74 us -> 81.3 us  [swap_blocks(): return lax.all_to_all(blocks, axis, split_axis=0, concat_axis=0, tiled=True)]
    unnamed x206 -> x212, local copies, waits for them, and re-layouts: 36.3 us -> 39 us
  transfers between devices with their start and end apart: 66 -> 67, of which waited for: 26 -> 26; matrix products, arithmetic and copies ran while one was open for 41% -> 42% of each run, Pallas kernels for 0% -> 0%
where the time goes in v3:
time: 1060 us; the launch traced here: 1050 us
  waiting for transfers between devices  371 us (35%)
  matrix products  233 us (22%)
  starting transfers between devices  187 us (18%)
  local copies, waits for them, and re-layouts  163 us (15%)
  other arithmetic  67.3 us (6%)
  between operations  28.7 us (3%)
    dot_general x35, matrix products, dot(): lax.dot_general(left, right, (((left_dim,), (right_dim,)), ((), ())), pre...  233 us
    all_to_all x14, waiting for transfers between devices, swap_blocks(): return lax.all_to_all(blocks, axis, split_axis=0, concat_axis=0, tiled=True)  136 us
    ppermute x16, waiting for transfers between devices, ring_scatter(): up, down = (lax.ppermute(up, F, right), lax.ppermute(down, F, left))  115 us
    all_to_all x14, starting transfers between devices, swap_blocks(): return lax.all_to_all(blocks, axis, split_axis=0, concat_axis=0, tiled=True)  81.3 us
    all_gather x1, waiting for transfers between devices, shards(): hidden_low = lax.all_gather(after(hidden_low, d_up), F, axis=0, tiled=True)  56.6 us
    ppermute x16, starting transfers between devices, ring_scatter(): up, down = (lax.ppermute(up, F, right), lax.ppermute(down, F, left))  52.8 us
    unnamed x212, local copies, waits for them, and re-layouts  39 us
    ppermute x12, waiting for transfers between devices, ring_gather(): up, down = (lax.ppermute(up, F, right), lax.ppermute(down, F, left))  35.8 us
  transfers between devices with their start and end apart: 67, of which 26 were waited for; matrix products, arithmetic and copies ran while one was open for 42% of the time, Pallas kernels for 0%

profile of v3, /device:TPU:1, one launch (start us, length us, event | category | flops | bytes accessed | tf_op | source)
XLA Modules:
  0.0 1049.5 jit_solution(647397215184211939)
XLA Ops:
  93.7 10.9 %all-to-all-start.2 = ((bf16[32,2,704]{2,1,0:T(2,128)(2,1)}), bf16[32,2,704]{2,1,0:T(2,128)(2,1)}, u32[]{:S(2)}, u32[]{:S(2)}) async-start(bf16[32,2,704]{2,1,0:T(2,128)(2,1)} %reshape.556), calls=%async_computation.2 | async-start | bytes 196608 | tf_op jit(solution)/shard_map/all_to_all | solution.py:153
  104.6 10.4 collective-permute-done.5
  146.3 10.9 %collective-permute-done.9 = bf16[512,768]{0,1:T(8,128)(2,1)S(1)} collective-permute-done((bf16[512,768]{0,1:T(8,128)(2,1)S(1)}, bf16[512,768]{0,1:T(8,128)(2,1)S(1)}, u32[]{:S(2)}, u32[]{:S(2)}) %collective-permute-start.9) | collective-permute-done | bytes 786464 | tf_op jit(solution)/shard_map/ppermute | solution.py:162
  180.0 100.6 %all-to-all-done.3 = bf16[8,1056,256]{2,1,0:T(8,128)(2,1)} async-done(((bf16[8,1056,256]{2,1,0:T(8,128)(2,1)}), bf16[8,1056,256]{2,1,0:T(8,128)(2,1)}, u32[]{:S(2)}, u32[]{:S(2)}) %all-to-all-start.3) | async-done | bytes 4325408 | tf_op jit(solution)/shard_map/all_to_all | solution.py:153
  299.0 13.4 %all-to-all-done.4 = bf16[8,128,256]{1,2,0:T(8,128)(2,1)S(1)} async-done(((bf16[8,128,256]{1,2,0:T(8,128)(2,1)}), bf16[8,128,256]{1,2,0:T(8,128)(2,1)S(1)}, u32[]{:S(2)}, u32[]{:S(2)}) %all-to-all-start.4) | async-done | bytes 524320 | tf_op jit(solution)/shard_map/all_to_all | solution.py:153
  317.2 12.3 %all-gather.11.cloned.1.call-start = ((), (), s32[]{:S(2)}) async-start(), calls=%async_computation.22 | async-start | bytes 6488064 | tf_op jit(solution)/shard_map/all_gather | solution.py:273
  420.1 15.5 %fusion.126 = f32[2048,1056]{0,1:T(8,128)} fusion(bf16[1056,2048]{1,0:T(8,128)(2,1)} %all-gather.9.cloned.1.call-done, bf16[1024,2048]{1,0:T(8,128)(2,1)} %collective-permute-done.19, bf16[1024,2048]{1,0:T(8,128)(2,1)} %constant_dynamic-update-slice_fusion.15), kind=kOutput, calls=%fused_computation.327 | convolution fusion | flops 8875147264 | bytes 21364736 | tf_op jit(solution)/shard_map/dot_general | solution.py:22
  435.6 15.9 %fusion.125 = f32[2048,1056]{0,1:T(8,128)} fusion(bf16[1056,2048]{1,0:T(8,128)(2,1)} %all-gather.11.cloned.1.call-done, bf16[1024,2048]{1,0:T(8,128)(2,1)} %collective-permute-done.19, bf16[1024,2048]{1,0:T(8,128)(2,1)} %constant_dynamic-update-slice_fusion.15), kind=kOutput, calls=%fused_computation.326 | convolution fusion | flops 8875147264 | bytes 21364736 | tf_op jit(solution)/shard_map/dot_general | solution.py:22
  451.7 12.0 %fusion = (bf16[2048,1056]{0,1:T(8,128)(2,1)S(1)}, bf16[2048,1056]{0,1:T(8,128)(2,1)}, f32[2048,1056]{0,1:T(8,128)}) fusion(f32[2048,1056]{0,1:T(8,128)} %fusion.125, f32[2048,1056]{0,1:T(8,128)} %fusion.126, f32[2048,12]{0,1:T(8,128)S(1)} %reshape.516, s32[1056]{0:T(1024)S(1)} %fusion.94), kind=kOutput, calls=%fused_computation.4 | convolution fusion | flops 330903936 | bytes 34705536 | tf_op jit(solution)/shard_map/dot_general | solution.py:22
  465.7 13.3 %convolution_convert_fusion.2 = bf16[1056,2048]{1,0:T(8,128)(2,1)} fusion(bf16[2048,1056]{0,1:T(8,128)(2,1)S(1)} %get-tuple-element.88, bf16[2048,2048]{1,0:T(8,128)(2,1)} %constant_dynamic-update-slice_fusion), kind=kOutput, calls=%fused_computation.20 | convolution fusion | flops 8860532736 | bytes 17039360 | tf_op jit(solution)/shard_map/dot_general | solution.py:22
  482.2 24.5 %multiply_convert_fusion = (bf16[2048,1056]{0,1:T(8,128)(2,1)}, bf16[2048,1056]{0,1:T(8,128)(2,1)}, f32[2048,1056]{0,1:T(8,128)}) fusion(f32[2048,1056]{0,1:T(8,128)} %get-tuple-element.342, f32[2048,1056]{0,1:T(8,128)} %fusion.126, f32[2048,1056]{0,1:T(8,128)} %fusion.125, bf16[2048,2048]{1,0:T(8,128)(2,1)} %constant_dynamic-update-slice_fusion, ...), kind=kOutput, calls=%fused_computation.6 | convolution fusion | flops 8888647680 | bytes 55967744 | tf_op jit(solution)/shard_map/dot_general | solution.py:22
  506.7 14.3 %convolution_convert_fusion.1 = bf16[1056,2048]{1,0:T(8,128)(2,1)} fusion(bf16[2048,1056]{0,1:T(8,128)(2,1)} %get-tuple-element.86, bf16[1024,2048]{1,0:T(8,128)(2,1)} %collective-permute-done.19, bf16[1024,2048]{1,0:T(8,128)(2,1)} %constant_dynamic-update-slice_fusion.15), kind=kOutput, calls=%fused_computation.19 | convolution fusion | flops 8877309952 | bytes 17039360 | tf_op jit(solution)/shard_map/dot_general | solution.py:22
  521.0 14.3 %convolution_convert_fusion = bf16[1056,2048]{1,0:T(8,128)(2,1)} fusion(bf16[2048,1056]{0,1:T(8,128)(2,1)} %get-tuple-element.87, bf16[1024,2048]{1,0:T(8,128)(2,1)} %collective-permute-done.19, bf16[1024,2048]{1,0:T(8,128)(2,1)} %constant_dynamic-update-slice_fusion.15), kind=kOutput, calls=%fused_computation.18 | convolution fusion | flops 8877309952 | bytes 17039360 | tf_op jit(solution)/shard_map/dot_general | solution.py:22
  535.4 8.5 fusion.18
  543.9 8.2 add_convert_fusion.2
  553.3 9.6 fusion.21
  563.0 10.6 %add_convert_fusion.1 = bf16[1024,2048]{1,0:T(8,128)(2,1)} fusion(bf16[1024,2048]{1,0:T(8,128)(2,1)S(1)} %collective-permute-done.21, f32[1024,2048]{1,0:T(8,128)} %fusion.21, bf16[1056,2048]{1,0:T(8,128)(2,1)S(1)} %bitcast.352, bf16[2048,1056]{0,1:T(8,128)(2,1)} %get-tuple-element.87), kind=kOutput, calls=%fused_computation.16 | convolution fusion | flops 4437573632 | bytes 23265280 | tf_op jit(solution)/shard_map/dot_general | solution.py:22
  573.6 7.7 convolution_convert_fusion.4
  581.4 8.1 fusion.1
  613.6 10.4 add_convert_fusion
  627.2 22.2 %collective-permute-done.28 = bf16[128,2048]{1,0:T(8,128)(2,1)S(1)} collective-permute-done((bf16[128,2048]{1,0:T(8,128)(2,1)S(1)}, bf16[128,2048]{1,0:T(8,128)(2,1)S(1)}, u32[]{:S(2)}, u32[]{:S(2)}) %collective-permute-start.28) | collective-permute-done | bytes 524320 | tf_op jit(solution)/shard_map/ppermute | solution.py:129
  655.1 9.0 collective-permute-start.30
  690.0 8.5 all-to-all-done.8
  712.9 8.6 multiply_reduce_fusion
  747.0 56.6 %all-gather.17.cloned.1.call-done = bf16[1024,2048]{1,0:T(8,128)(2,1)} async-done(((bf16[128,2048]{1,0:T(8,128)(2,1)}), bf16[1024,2048]{1,0:T(8,128)(2,1)}) %all-gather.17.cloned.1.call-update) | async-done | bytes 4194320 | tf_op jit(solution)/shard_map/all_gather | solution.py:457
  834.5 38.7 %collective-permute-done.32 = bf16[64,2048]{1,0:T(8,128)(2,1)S(1)} collective-permute-done((bf16[64,2048]{1,0:T(8,128)(2,1)S(1)}, bf16[64,2048]{1,0:T(8,128)(2,1)S(1)}, u32[]{:S(2)}, u32[]{:S(2)}) %collective-permute-start.32) | collective-permute-done | bytes 262176 | tf_op jit(solution)/shard_map/ppermute | solution.py:129
  874.5 20.5 %collective-permute-start.34 = (bf16[128,2048]{1,0:T(8,128)(2,1)S(1)}, bf16[128,2048]{1,0:T(8,128)(2,1)S(1)}, u32[]{:S(2)}, u32[]{:S(2)}) collective-permute-start(bf16[128,2048]{1,0:T(8,128)(2,1)S(1)} %pad_maximum_fusion.12), channel_id=1, source_target_pairs={{0,2},{2,4},{4,6},{6,7},{7,5},{5,3},{3,1},{1,0},{8,10},{10,12},{12... | collective-permute-start | bytes 1572872 | tf_op jit(solution)/shard_map/ppermute | solution.py:129
  895.0 21.8 %collective-permute-done.34 = bf16[128,2048]{1,0:T(8,128)(2,1)S(1)} collective-permute-done((bf16[128,2048]{1,0:T(8,128)(2,1)S(1)}, bf16[128,2048]{1,0:T(8,128)(2,1)S(1)}, u32[]{:S(2)}, u32[]{:S(2)}) %collective-permute-start.34) | collective-permute-done | bytes 524320 | tf_op jit(solution)/shard_map/ppermute | solution.py:129
  918.7 10.2 collective-permute-start.35
  971.1 10.8 %all-to-all-start.13 = ((bf16[4,128,1408]{2,1,0:T(8,128)(2,1)}), bf16[4,128,1408]{2,1,0:T(8,128)(2,1)}, u32[]{:S(2)}, u32[]{:S(2)}) async-start(bf16[4,128,1408]{2,1,0:T(8,128)(2,1)} %bitcast.291), calls=%async_computation.19 | async-start | bytes 2883584 | tf_op jit(solution)/shard_map/all_to_all | solution.py:153
  983.1 12.7 %collective-permute-done.39 = bf16[128,2048]{1,0:T(8,128)(2,1)} collective-permute-done((bf16[128,2048]{1,0:T(8,128)(2,1)}, bf16[128,2048]{1,0:T(8,128)(2,1)}, u32[]{:S(2)}, u32[]{:S(2)}) %collective-permute-start.39) | collective-permute-done | bytes 524320 | tf_op jit(solution)/shard_map/ppermute | solution.py:137
  1029.5 8.7 collective-permute-done.40
  (597 shorter events, 461.0 us)
Async XLA Ops:
  7.2 322.4 %all-gather.7.cloned.1.call-start = ((), (), s32[]{:S(2)}) async-start(), calls=%async_computation.20 | async-start | bytes 8650752 | tf_op jit(solution)/shard_map/all_gather | solution.py:237
  14.2 45.7 %all-to-all-start.1 = ((bf16[4,128,1408]{2,1,0:T(8,128)(2,1)}), bf16[4,128,1408]{2,1,0:T(8,128)(2,1)S(1)}, u32[]{:S(2)}, u32[]{:S(2)}) async-start(bf16[4,128,1408]{2,1,0:T(8,128)(2,1)} %bitcast.333), calls=%async_computation.1 | async-start | bytes 2883584 | tf_op jit(solution)/shard_map/all_to_all | solution.py:153
  38.4 31.0 %collective-permute-start.2 = (bf16[128,2048]{1,0:T(8,128)(2,1)}, bf16[128,2048]{1,0:T(8,128)(2,1)}, u32[]{:S(2)}, u32[]{:S(2)}) collective-permute-start(bf16[128,2048]{1,0:T(8,128)(2,1)} %collective-permute-done), channel_id=1, source_target_pairs={{0,2},{2,4},{4,6},{6,7},{7,5},{5,3},{3,1},{1,0},{8,10},{10,12},{12... | collective-permute-start | bytes 1572872 | tf_op jit(solution)/shard_map/ppermute | solution.py:106
  59.9 33.8 %all-to-all-start = ((bf16[8,64,768]{2,1,0:T(8,128)(2,1)}), bf16[8,64,768]{2,1,0:T(8,128)(2,1)S(1)}, u32[]{:S(2)}, u32[]{:S(2)}) async-start(bf16[8,64,768]{2,1,0:T(8,128)(2,1)} %bitcast.3), calls=%async_computation | async-start | bytes 1572864 | tf_op jit(solution)/shard_map/all_to_all | solution.py:153
  69.4 35.2 %collective-permute-start.4 = (bf16[128,2048]{1,0:T(8,128)(2,1)}, bf16[128,2048]{1,0:T(8,128)(2,1)}, u32[]{:S(2)}, u32[]{:S(2)}) collective-permute-start(bf16[128,2048]{1,0:T(8,128)(2,1)} %collective-permute-done.2), channel_id=1, source_target_pairs={{0,2},{2,4},{4,6},{6,7},{7,5},{5,3},{3,1},{1,0},{8,10},{10,12},{12... | collective-permute-start | bytes 1572872 | tf_op jit(solution)/shard_map/ppermute | solution.py:106
  71.0 44.1 %collective-permute-start.5 = (bf16[128,2048]{1,0:T(8,128)(2,1)}, bf16[128,2048]{1,0:T(8,128)(2,1)}, u32[]{:S(2)}, u32[]{:S(2)}) collective-permute-start(bf16[128,2048]{1,0:T(8,128)(2,1)} %collective-permute-done.3), channel_id=1, source_target_pairs={{0,1},{2,0},{4,2},{6,4},{7,6},{5,7},{3,5},{1,3},{8,9},{10,8},{12,1... | collective-permute-start | bytes 1572872 | tf_op jit(solution)/shard_map/ppermute | solution.py:106
  93.7 37.5 %all-to-all-start.2 = ((bf16[32,2,704]{2,1,0:T(2,128)(2,1)}), bf16[32,2,704]{2,1,0:T(2,128)(2,1)}, u32[]{:S(2)}, u32[]{:S(2)}) async-start(bf16[32,2,704]{2,1,0:T(2,128)(2,1)} %reshape.556), calls=%async_computation.2 | async-start | bytes 196608 | tf_op jit(solution)/shard_map/all_to_all | solution.py:153
  131.2 149.4 %all-to-all-start.3 = ((bf16[8,1056,256]{2,1,0:T(8,128)(2,1)}), bf16[8,1056,256]{2,1,0:T(8,128)(2,1)}, u32[]{:S(2)}, u32[]{:S(2)}) async-start(bf16[8,1056,256]{2,1,0:T(8,128)(2,1)} %pad_maximum_fusion.1), calls=%async_computation.3 | async-start | bytes 8650752 | tf_op jit(solution)/shard_map/all_to_all | solution.py:153
  136.0 226.5 %all-gather.15.cloned.1.call-start = ((), (), s32[]{:S(2)}) async-start(), calls=%async_computation.24 | async-start | bytes 4718592 | tf_op jit(solution)/shard_map/all_gather | solution.py:303
  136.7 283.4 %all-gather.9.cloned.1.call-start = ((), (), s32[]{:S(2)}) async-start(), calls=%async_computation.21 | async-start | bytes 6488064 | tf_op jit(solution)/shard_map/all_gather | solution.py:273
  312.4 67.9 %all-to-all-start.5 = ((bf16[8,352,256]{2,1,0:T(8,128)(2,1)}), bf16[8,352,256]{2,1,0:T(8,128)(2,1)S(1)}, u32[]{:S(2)}, u32[]{:S(2)}) async-start(bf16[8,352,256]{2,1,0:T(8,128)(2,1)} %bitcast.28), calls=%async_computation.5 | async-start | bytes 2883584 | tf_op jit(solution)/shard_map/all_to_all | solution.py:153
  317.2 118.4 %all-gather.11.cloned.1.call-start = ((), (), s32[]{:S(2)}) async-start(), calls=%async_computation.22 | async-start | bytes 6488064 | tf_op jit(solution)/shard_map/all_gather | solution.py:273
  362.4 47.9 %collective-permute-start.20 = (bf16[1024,2048]{1,0:T(8,128)(2,1)}, bf16[1024,2048]{1,0:T(8,128)(2,1)}, u32[]{:S(2)}, u32[]{:S(2)}) collective-permute-start(bf16[1024,2048]{1,0:T(8,128)(2,1)} %all-gather.15.cloned.1.call-done), channel_id=1, source_target_pairs={{0,8},{8,0},{16,24},{24,16},{1,9},{9,1},{17,25},{25,17},{2,10},{10... | collective-permute-start | bytes 12582920 | tf_op jit(solution)/shard_map/ppermute | solution.py:157
  364.4 117.9 %all-gather.13.cloned.1.call-start = ((), (), s32[]{:S(2)}) async-start(), calls=%async_computation.23 | async-start | bytes 6488064 | tf_op jit(solution)/shard_map/all_gather | solution.py:273
  410.3 196.8 %reduce-scatter.7.cloned.1.call-start = ((), (), s32[]{:S(2)}) async-start(), calls=%async_computation.25 | async-start | bytes 6488064 | tf_op jit(solution)/shard_map/reduce_scatter | solution.py:383
  479.0 210.1 %reduce-scatter.9.cloned.1.call-start = ((), (), s32[]{:S(2)}) async-start(), calls=%async_computation.26 | async-start | bytes 6488064 | tf_op jit(solution)/shard_map/reduce_scatter | solution.py:383
  535.3 186.2 %reduce-scatter.17.cloned.1.call-start = ((), (), s32[]{:S(2)}) async-start(), calls=%async_computation.31 | async-start | bytes 6488064 | tf_op jit(solution)/shard_map/reduce_scatter | solution.py:383
  610.0 42.9 %all-to-all-start.7 = ((bf16[8,352,256]{2,1,0:T(8,128)(2,1)}), bf16[8,352,256]{2,1,0:T(8,128)(2,1)S(1)}, u32[]{:S(2)}, u32[]{:S(2)}) async-start(bf16[8,352,256]{2,1,0:T(8,128)(2,1)} %bitcast.293), calls=%async_computation.8 | async-start | bytes 2883584 | tf_op jit(solution)/shard_map/all_to_all | solution.py:153
  689.0 114.6 %all-gather.17.cloned.1.call-start = ((), (), s32[]{:S(2)}) async-start(), calls=%async_computation.27 | async-start | bytes 4718592 | tf_op jit(solution)/shard_map/all_gather | solution.py:457
  689.7 239.1 %reduce-scatter.13.cloned.1.call-start = ((), (), s32[]{:S(2)}) async-start(), calls=%async_computation.29 | async-start | bytes 3932160 | tf_op jit(solution)/shard_map/reduce_scatter | solution.py:496
  739.2 74.8 %all-to-all-start.11 = ((bf16[8,528,256]{2,1,0:T(8,128)(2,1)}), bf16[8,528,256]{2,1,0:T(8,128)(2,1)}, u32[]{:S(2)}, u32[]{:S(2)}) async-start(bf16[8,528,256]{2,1,0:T(8,128)(2,1)} %pad_maximum_fusion.5), calls=%async_computation.17 | async-start | bytes 4325376 | tf_op jit(solution)/shard_map/all_to_all | solution.py:153
  746.7 274.8 %reduce-scatter.15.cloned.1.call-start = ((), (), s32[]{:S(2)}) async-start(), calls=%async_computation.30 | async-start | bytes 1310720 | tf_op jit(solution)/shard_map/reduce_scatter | solution.py:494
  808.1 231.0 %reduce-scatter.11.cloned.1.call-start = ((), (), s32[]{:S(2)}) async-start(), calls=%async_computation.28 | async-start | bytes 4718592 | tf_op jit(solution)/shard_map/reduce_scatter | solution.py:458
  826.2 105.0 %all-to-all-start.12 = ((bf16[8,528,256]{2,1,0:T(8,128)(2,1)}), bf16[8,528,256]{2,1,0:T(8,128)(2,1)}, u32[]{:S(2)}, u32[]{:S(2)}) async-start(bf16[8,528,256]{2,1,0:T(8,128)(2,1)} %pad_maximum_fusion.6), calls=%async_computation.18 | async-start | bytes 4325376 | tf_op jit(solution)/shard_map/all_to_all | solution.py:153
  832.9 40.3 %collective-permute-start.32 = (bf16[64,2048]{1,0:T(8,128)(2,1)S(1)}, bf16[64,2048]{1,0:T(8,128)(2,1)S(1)}, u32[]{:S(2)}, u32[]{:S(2)}) collective-permute-start(bf16[64,2048]{1,0:T(8,128)(2,1)S(1)} %get-tuple-element.237), channel_id=1, source_target_pairs={{0,2},{2,4},{4,6},{6,7},{7,5},{5,3},{3,1},{1,0},{8,10},{10,12},{12... | collective-permute-start | bytes 786440 | tf_op jit(solution)/shard_map/ppermute | solution.py:129
  834.4 38.8 %collective-permute-start.33 = (bf16[64,2048]{1,0:T(8,128)(2,1)S(1)}, bf16[64,2048]{1,0:T(8,128)(2,1)S(1)}, u32[]{:S(2)}, u32[]{:S(2)}) collective-permute-start(bf16[64,2048]{1,0:T(8,128)(2,1)S(1)} %get-tuple-element.238), channel_id=1, source_target_pairs={{0,1},{2,0},{4,2},{6,4},{7,6},{5,7},{3,5},{1,3},{8,9},{10,8},{12,1... | collective-permute-start | bytes 786440 | tf_op jit(solution)/shard_map/ppermute | solution.py:129
  874.5 42.3 %collective-permute-start.34 = (bf16[128,2048]{1,0:T(8,128)(2,1)S(1)}, bf16[128,2048]{1,0:T(8,128)(2,1)S(1)}, u32[]{:S(2)}, u32[]{:S(2)}) collective-permute-start(bf16[128,2048]{1,0:T(8,128)(2,1)S(1)} %pad_maximum_fusion.12), channel_id=1, source_target_pairs={{0,2},{2,4},{4,6},{6,7},{7,5},{5,3},{3,1},{1,0},{8,10},{10,12},{12... | collective-permute-start | bytes 1572872 | tf_op jit(solution)/shard_map/ppermute | solution.py:129
  895.0 41.0 %collective-permute-start.37 = (bf16[128,2048]{1,0:T(8,128)(2,1)S(1)}, bf16[128,2048]{1,0:T(8,128)(2,1)}, u32[]{:S(2)}, u32[]{:S(2)}) collective-permute-start(bf16[128,2048]{1,0:T(8,128)(2,1)S(1)} %pad_maximum_fusion.13), channel_id=1, source_target_pairs={{0,1},{2,0},{4,2},{6,4},{7,6},{5,7},{3,5},{1,3},{8,9},{10,8},{12,1... | collective-permute-start | bytes 1572872 | tf_op jit(solution)/shard_map/ppermute | solution.py:129
  931.2 40.0 %all-to-all-start.9 = ((bf16[8,64,768]{2,1,0:T(8,128)(2,1)}), bf16[8,64,768]{2,1,0:T(8,128)(2,1)S(1)}, u32[]{:S(2)}, u32[]{:S(2)}) async-start(bf16[8,64,768]{2,1,0:T(8,128)(2,1)} %bitcast.75), calls=%async_computation.13 | async-start | bytes 1572864 | tf_op jit(solution)/shard_map/all_to_all | solution.py:153
  949.5 33.6 %collective-permute-start.36 = (bf16[128,2048]{1,0:T(8,128)(2,1)}, bf16[128,2048]{1,0:T(8,128)(2,1)}, u32[]{:S(2)}, u32[]{:S(2)}) collective-permute-start(bf16[128,2048]{1,0:T(8,128)(2,1)} %get-tuple-element.234), channel_id=1, source_target_pairs={{0,2},{2,4},{4,6},{6,7},{7,5},{5,3},{3,1},{1,0},{8,10},{10,12},{12... | collective-permute-start | bytes 1572872 | tf_op jit(solution)/shard_map/ppermute | solution.py:137
  960.0 35.7 %collective-permute-start.39 = (bf16[128,2048]{1,0:T(8,128)(2,1)}, bf16[128,2048]{1,0:T(8,128)(2,1)}, u32[]{:S(2)}, u32[]{:S(2)}) collective-permute-start(bf16[128,2048]{1,0:T(8,128)(2,1)} %add_convert_fusion.3), channel_id=1, source_target_pairs={{0,1},{2,0},{4,2},{6,4},{7,6},{5,7},{3,5},{1,3},{8,9},{10,8},{12,1... | collective-permute-start | bytes 1572872 | tf_op jit(solution)/shard_map/ppermute | solution.py:137
  971.1 52.3 %all-to-all-start.13 = ((bf16[4,128,1408]{2,1,0:T(8,128)(2,1)}), bf16[4,128,1408]{2,1,0:T(8,128)(2,1)}, u32[]{:S(2)}, u32[]{:S(2)}) async-start(bf16[4,128,1408]{2,1,0:T(8,128)(2,1)} %bitcast.291), calls=%async_computation.19 | async-start | bytes 2883584 | tf_op jit(solution)/shard_map/all_to_all | solution.py:153
  (132 other events, 2294.7 us)
Sparse Core Ops, SparseCore 0:
  11.6 105.6 all-gather.6
  139.0 139.5 all-gather.14
  286.2 59.6 all-gather.8
  364.5 57.4 all-gather.10
  424.0 58.2 all-gather.12
  484.4 55.7 reduce-scatter.6
  542.6 55.7 reduce-scatter.8
  600.6 55.7 reduce-scatter.16
  692.8 110.7 all-gather.16
  806.1 36.8 reduce-scatter.12
  845.6 24.8 reduce-scatter.14
  874.4 122.4 reduce-scatter.10
